TPU v7x, 32 devices: a whole 2x2x4 slice. The times are simulated.
32 devices in a mesh: samp: 16 (over z, y, core), blk: 2 (over x).
Axes of the slice: x: 2, y: 2, z: 4, core: 2. Of those that a mesh axis runs over, the one named last changes fastest.
Arguments:
- activations: bfloat16 [16, 1024, 768], P('samp', 'blk'), may hold values from -6 to 6
- single_cond: bfloat16 [2, 1024, 384], P(None, 'blk'), may hold values from -6 to 6
- pair_repr: bfloat16 [2, 1024, 1024, 128], P(None, 'blk', 'samp'), may hold values from -6 to 6
- struct_id: int32 [16], P('samp'), may hold values from 0 to 1, as said below
- seq_lengths: int32 [2], replicated, may hold values from 513 to 1024, as said below
- qkvg_weight: bfloat16 [768, 3072], replicated, may hold values from -0.21875 to 0.21875
- query_bias: float32 [768], replicated, may hold values from -4 to 4
- out_weight: bfloat16 [768, 768], replicated, may hold values from -3.5 to 3.5
- in_weight: bfloat16 [768, 3072], replicated, may hold values from -0.21875 to 0.21875
- down_weight: bfloat16 [1536, 768], replicated, may hold values from -0.3125 to 0.3125
- cond_weight: bfloat16 [2, 384, 2304], replicated, may hold values from -0.3125 to 0.3125
- cond_bias: float32 [2, 1536], replicated, may hold values from -4 to 4
- single_gain: float32 [2, 384], replicated, may hold values from 0.1 to 1.9
- pair_gain: float32 [128], replicated, may hold values from 0.1 to 1.9
- pair_weight: bfloat16 [128, 16], replicated, may hold values from -0.5 to 0.5
- cotangent: bfloat16 [16, 1024, 768], P('samp', 'blk'), may hold values from -6 to 6
Outputs:
- block_out: bfloat16 [16, 1024, 768], P('samp', 'blk')
- act_grad: float32 [16, 1024, 768], P('samp', 'blk')
- single_grad: float32 [2, 1024, 384], P(None, 'blk')
- pair_grad: float32 [2, 1024, 1024, 128], P(None, 'blk', 'samp')
- qkvg_grad: float32 [768, 3072], P('samp', 'blk')
- query_bias_grad: float32 [768], replicated
- out_grad: float32 [768, 768], P('samp', 'blk')
- in_grad: float32 [768, 3072], P('samp', 'blk')
- down_grad: float32 [1536, 768], P('samp', 'blk')
- cond_grad: float32 [2, 384, 2304], P(None, 'samp', 'blk')
- cond_bias_grad: float32 [2, 1536], replicated
- single_gain_grad: float32 [2, 384], replicated
- pair_gain_grad: float32 [128], replicated
- pair_weight_grad: float32 [128, 16], replicated
Inputs may be any that keep to these rules, and one draw needn't show every extreme that they name: `struct_id`: exactly 8 samples belong to each of the two structures. `seq_lengths`: one structure, drawn from the seed, has all 1024 tokens.
All inputs are finite; a program needn't handle non-finite values.
Results may differ from a plain program's by a relative error of at most 0.023.
Values may be sent and summed in bfloat16 or wider, within the bound.
No kernel may reach another device: no remote copies, remote signals or barrier semaphores. Data moves between devices by JAX's collectives and lax.ppermute only.
A program may use at most 384 MiB of HBM per device.

v0:
```python
import math

import jax
import jax.numpy as jnp
from jax import lax
from jax.sharding import PartitionSpec as P

EPS = 1e-05
MASKED = -1000000000.0


def norm_rows(value):
    center = value - jnp.mean(value, axis=-1, keepdims=True)
    return center * lax.rsqrt(jnp.mean(center * center, axis=-1, keepdims=True) + EPS)


def pick_struct(table, ids):
    expand = (ids.shape[0],) + (1,) * (table.ndim - 1)
    chosen = jnp.broadcast_to(table[0][None], (ids.shape[0],) + table.shape[1:])
    chosen = jnp.where(ids.reshape(expand) == 1, table[1][None], chosen)
    return chosen


def struct_sum(values, ids, structs):
    expand = (ids.shape[0],) + (1,) * (values.ndim - 1)
    return jnp.stack(
        [
            jnp.sum(jnp.where(ids.reshape(expand) == member, values, 0.0), axis=0)
            for member in range(structs)
        ]
    )


def block_length(piece_len):
    return math.gcd(piece_len, 512)


def local(
    activations,
    single_cond,
    pair_repr,
    struct_id,
    seq_lengths,
    qkvg_weight,
    query_bias,
    out_weight,
    in_weight,
    down_weight,
    cond_weight,
    cond_bias,
    single_gain,
    pair_gain,
    pair_weight,
    cotangent,
):
    samples_dev, tok_rows, width = activations.shape
    heads = pair_weight.shape[1]
    head_dim = width // heads
    hidden_units = down_weight.shape[0]
    structs = single_cond.shape[0]
    seq_total = tok_rows * lax.axis_size("blk")
    score_scale = 1.0 / math.sqrt(head_dim)
    zero_index = jnp.zeros((), jnp.int32)
    key_limit = pick_struct(seq_lengths, struct_id)
    single_hat = norm_rows(single_cond.astype(jnp.float32))
    cond_inputs = []
    cond_rows = []
    for sublayer in range(2):
        cond_in = (single_hat * single_gain[sublayer]).astype(jnp.bfloat16)
        bias_row = jnp.concatenate(
            [
                cond_bias[sublayer, :width],
                jnp.zeros((width,), jnp.float32),
                cond_bias[sublayer, width:],
            ]
        )
        cond_pre = (
            jnp.einsum(
                "cti,ij->ctj", cond_in, cond_weight[sublayer], preferred_element_type=jnp.float32
            )
            + bias_row
        )
        cond_inputs.append(cond_in)
        cond_rows.append(pick_struct(cond_pre, struct_id))
    pair_hat, pair_norm_back = jax.vjp(norm_rows, pair_repr.astype(jnp.float32))
    pair_in = (pair_hat * pair_gain).astype(jnp.bfloat16)
    bias_local = jnp.einsum(
        "crkz,zh->crhk", pair_in, pair_weight, preferred_element_type=jnp.float32
    ).astype(jnp.bfloat16)
    bias_all = lax.all_gather(bias_local, "samp", axis=3, tiled=True)
    act_float = activations.astype(jnp.float32)
    act_hat, act_norm_back = jax.vjp(norm_rows, act_float)
    cond_attn = cond_rows[0]
    scale_attn = jax.nn.sigmoid(cond_attn[..., :width])
    gate_attn = jax.nn.sigmoid(cond_attn[..., 2 * width :])
    x_attn = (scale_attn * act_hat + cond_attn[..., width : 2 * width]).astype(jnp.bfloat16)
    proj_bias = jnp.concatenate([query_bias, jnp.zeros((3 * width,), jnp.float32)])
    projected = (
        jnp.einsum("sti,ij->stj", x_attn, qkvg_weight, preferred_element_type=jnp.float32)
        + proj_bias
    )
    query = (
        projected[..., :width].astype(jnp.bfloat16).reshape(samples_dev, tok_rows, heads, head_dim)
    )
    keys_values = projected[..., width : 3 * width].astype(jnp.bfloat16)
    gate_pre = projected[..., 3 * width :]

    def block_scores(sub_kv, offset):
        block_len = sub_kv.shape[1]
        keys_block = sub_kv[..., :width].reshape(samples_dev, block_len, heads, head_dim)
        scores = (
            jnp.einsum("sqhd,skhd->sqhk", query, keys_block, preferred_element_type=jnp.float32)
            * score_scale
        )
        bias_block = lax.dynamic_slice_in_dim(bias_all, offset, block_len, 3)
        scores = scores + pick_struct(bias_block, struct_id).astype(jnp.float32)
        positions = offset + jnp.arange(block_len, dtype=jnp.int32)
        valid = positions[None, :] < key_limit[:, None]
        return jnp.where(valid[:, None, None, :], scores, MASKED)

    def forward_fold(state, block_kv):
        block_len = block_length(block_kv.shape[1])
        count = block_kv.shape[1] // block_len

        def forward_step(carry, index):
            row_peak, row_total, row_acc = carry
            sub_offset = index * block_len
            sub_kv = lax.dynamic_slice_in_dim(block_kv, index * block_len, block_len, 1)
            scores = block_scores(sub_kv, sub_offset)
            values_block = sub_kv[..., width:].reshape(samples_dev, block_len, heads, head_dim)
            new_peak = jnp.maximum(row_peak, jnp.max(scores, axis=-1))
            rescale = jnp.exp(row_peak - new_peak)
            weights = jnp.exp(scores - new_peak[..., None])
            row_total = row_total * rescale + jnp.sum(weights, axis=-1)
            row_acc = row_acc * rescale[..., None] + jnp.einsum(
                "sqhk,skhd->sqhd",
                weights.astype(jnp.bfloat16),
                values_block,
                preferred_element_type=jnp.float32,
            )
            return ((new_peak, row_total, row_acc), None)

        result, ignored = lax.scan(
            jax.checkpoint(forward_step), state, jnp.arange(count, dtype=jnp.int32)
        )
        return result

    stats_shape = (samples_dev, tok_rows, heads)
    forward_init = (
        jnp.full(stats_shape, -1e30, jnp.float32),
        jnp.zeros(stats_shape, jnp.float32),
        jnp.zeros((samples_dev, tok_rows, heads, head_dim), jnp.float32),
    )
    row_peak, row_total, row_acc = forward_fold(
        forward_init, lax.all_gather(keys_values, "blk", axis=1, tiled=True)
    )
    attn4 = row_acc / row_total[..., None]
    log_sum = row_peak + jnp.log(row_total)
    attn = attn4.reshape(samples_dev, tok_rows, width)
    gate_val = jax.nn.sigmoid(gate_pre)
    mixed = (gate_val * attn).astype(jnp.bfloat16)
    att_out = jnp.einsum("sti,ij->stj", mixed, out_weight, preferred_element_type=jnp.float32)
    hidden_state = act_float + gate_attn * att_out
    cond_trans = cond_rows[1]
    scale_trans = jax.nn.sigmoid(cond_trans[..., :width])
    gate_trans = jax.nn.sigmoid(cond_trans[..., 2 * width :])
    hidden_hat, hidden_norm_back = jax.vjp(norm_rows, hidden_state)
    x_trans = (scale_trans * hidden_hat + cond_trans[..., width : 2 * width]).astype(jnp.bfloat16)
    up_proj = jnp.einsum("sti,ij->stj", x_trans, in_weight, preferred_element_type=jnp.float32)
    up_gate = up_proj[..., :hidden_units]
    up_lin = up_proj[..., hidden_units:]
    sig_gate = jax.nn.sigmoid(up_gate)
    silu_gate = up_gate * sig_gate
    hidden_act = (silu_gate * up_lin).astype(jnp.bfloat16)
    trans = jnp.einsum("stf,fd->std", hidden_act, down_weight, preferred_element_type=jnp.float32)
    block_out = (hidden_state + gate_trans * trans).astype(jnp.bfloat16)
    d_out = cotangent.astype(jnp.float32)
    d_trans = (gate_trans * d_out).astype(jnp.bfloat16)
    grad_down = jnp.einsum("stf,std->fd", hidden_act, d_trans, preferred_element_type=jnp.float32)
    d_hid = jnp.einsum("std,fd->stf", d_trans, down_weight, preferred_element_type=jnp.float32)
    silu_slope = sig_gate * (1.0 + up_gate * (1.0 - sig_gate))
    d_up = jnp.concatenate([d_hid * up_lin * silu_slope, d_hid * silu_gate], axis=-1).astype(
        jnp.bfloat16
    )
    grad_in = jnp.einsum("sti,stj->ij", x_trans, d_up, preferred_element_type=jnp.float32)
    d_xt = jnp.einsum("stj,ij->sti", d_up, in_weight, preferred_element_type=jnp.float32)
    d_hidden = d_out + hidden_norm_back(d_xt * scale_trans)[0]
    d_cond_trans = jnp.concatenate(
        [
            d_xt * hidden_hat * scale_trans * (1.0 - scale_trans),
            d_xt,
            d_out * trans * gate_trans * (1.0 - gate_trans),
        ],
        axis=-1,
    )
    d_att = (gate_attn * d_hidden).astype(jnp.bfloat16)
    grad_out = jnp.einsum("sti,stj->ij", mixed, d_att, preferred_element_type=jnp.float32)
    d_mixed = jnp.einsum("stj,ij->sti", d_att, out_weight, preferred_element_type=jnp.float32)
    d_attn = (gate_val * d_mixed).astype(jnp.bfloat16)
    d_gate_pre = d_mixed * attn * gate_val * (1.0 - gate_val)
    d_attn4 = d_attn.reshape(samples_dev, tok_rows, heads, head_dim)
    row_delta = jnp.sum(d_attn4.astype(jnp.float32) * attn4, axis=-1)

    def backward_fold(state, block_kv):
        block_len = block_length(block_kv.shape[1])
        count = block_kv.shape[1] // block_len

        def backward_step(carry, index):
            d_query, d_kv, d_bias = carry
            sub_offset = index * block_len
            sub_kv = lax.dynamic_slice_in_dim(block_kv, index * block_len, block_len, 1)
            keys_block = sub_kv[..., :width].reshape(samples_dev, block_len, heads, head_dim)
            values_block = sub_kv[..., width:].reshape(samples_dev, block_len, heads, head_dim)
            scores = block_scores(sub_kv, sub_offset)
            attn_probs = jnp.exp(scores - log_sum[..., None])
            d_probs = jnp.einsum(
                "sqhd,skhd->sqhk", d_attn4, values_block, preferred_element_type=jnp.float32
            )
            d_scores = (attn_probs * (d_probs - row_delta[..., None])).astype(jnp.bfloat16)
            d_query = (
                d_query
                + jnp.einsum(
                    "sqhk,skhd->sqhd", d_scores, keys_block, preferred_element_type=jnp.float32
                )
                * score_scale
            )
            d_keys = (
                jnp.einsum("sqhk,sqhd->skhd", d_scores, query, preferred_element_type=jnp.float32)
                * score_scale
            )
            d_values = jnp.einsum(
                "sqhk,sqhd->skhd",
                attn_probs.astype(jnp.bfloat16),
                d_attn4,
                preferred_element_type=jnp.float32,
            )
            d_new = jnp.concatenate(
                [
                    d_keys.reshape(samples_dev, block_len, width),
                    d_values.reshape(samples_dev, block_len, width),
                ],
                axis=-1,
            )
            d_kv = lax.dynamic_update_slice(d_kv, d_new, (zero_index, sub_offset, zero_index))
            bias_part = struct_sum(d_scores.astype(jnp.float32), struct_id, structs)
            d_bias = lax.dynamic_update_slice(
                d_bias, bias_part, (zero_index, zero_index, zero_index, sub_offset)
            )
            return ((d_query, d_kv, d_bias), None)

        result, ignored = lax.scan(
            jax.checkpoint(backward_step), state, jnp.arange(count, dtype=jnp.int32)
        )
        return result

    backward_init = (
        jnp.zeros((samples_dev, tok_rows, heads, head_dim), jnp.float32),
        jnp.zeros((samples_dev, seq_total, 2 * width), jnp.float32),
        jnp.zeros((structs, tok_rows, heads, seq_total), jnp.float32),
    )
    d_query, d_kv, d_bias = backward_fold(
        backward_init, lax.all_gather(keys_values, "blk", axis=1, tiled=True)
    )
    d_kv_own = lax.psum_scatter(
        d_kv.astype(jnp.bfloat16), "blk", scatter_dimension=1, tiled=True
    ).astype(jnp.float32)
    d_proj = jnp.concatenate(
        [d_query.reshape(samples_dev, tok_rows, width), d_kv_own, d_gate_pre], axis=-1
    ).astype(jnp.bfloat16)
    grad_qkvg = jnp.einsum("sti,stj->ij", x_attn, d_proj, preferred_element_type=jnp.float32)
    grad_query_bias = jnp.sum(d_proj[..., :width].astype(jnp.float32), axis=(0, 1))
    d_xa = jnp.einsum("stj,ij->sti", d_proj, qkvg_weight, preferred_element_type=jnp.float32)
    act_grad = d_hidden + act_norm_back(d_xa * scale_attn)[0]
    d_cond_attn = jnp.concatenate(
        [
            d_xa * act_hat * scale_attn * (1.0 - scale_attn),
            d_xa,
            d_hidden * att_out * gate_attn * (1.0 - gate_attn),
        ],
        axis=-1,
    )
    d_cond_all = jnp.concatenate(
        [struct_sum(d_cond_attn, struct_id, structs), struct_sum(d_cond_trans, struct_id, structs)],
        axis=-1,
    )
    bias_sum, cond_sum = (
        lax.psum_scatter(
            d_bias.astype(jnp.bfloat16), "samp", scatter_dimension=3, tiled=True
        ).astype(jnp.float32),
        lax.psum_scatter(
            d_cond_all.astype(jnp.bfloat16), "samp", scatter_dimension=1, tiled=True
        ).astype(jnp.float32),
    )
    bias_round = bias_sum.astype(jnp.bfloat16)
    grad_pair_weight = jnp.einsum(
        "crkz,crhk->zh", pair_in, bias_round, preferred_element_type=jnp.float32
    )
    d_pair_in = jnp.einsum(
        "crhk,zh->crkz", bias_round, pair_weight, preferred_element_type=jnp.float32
    )
    grad_pair_gain = jnp.sum(d_pair_in * pair_hat, axis=(0, 1, 2))
    pair_grad = pair_norm_back(d_pair_in * pair_gain)[0]
    slice_len = cond_sum.shape[1]
    slice_start = lax.axis_index("samp") * slice_len
    single_part = lax.dynamic_slice_in_dim(single_cond, slice_start, slice_len, 1).astype(
        jnp.float32
    )
    part_hat, part_norm_back = jax.vjp(norm_rows, single_part)
    cond_round = cond_sum.astype(jnp.bfloat16)
    d_part_hat = jnp.zeros_like(part_hat)
    cond_grads = []
    cond_bias_grads = []
    gain_grads = []
    for sublayer in range(2):
        d_layer = cond_round[..., sublayer * 3 * width : (sublayer + 1) * 3 * width]
        part_in = lax.dynamic_slice_in_dim(cond_inputs[sublayer], slice_start, slice_len, 1)
        cond_grads.append(
            jnp.einsum("cti,ctj->ij", part_in, d_layer, preferred_element_type=jnp.float32)
        )
        layer_sums = jnp.sum(d_layer.astype(jnp.float32), axis=(0, 1))
        cond_bias_grads.append(jnp.concatenate([layer_sums[:width], layer_sums[2 * width :]]))
        d_in = jnp.einsum(
            "ctj,ij->cti", d_layer, cond_weight[sublayer], preferred_element_type=jnp.float32
        )
        gain_grads.append(jnp.sum(d_in * part_hat, axis=(0, 1)))
        d_part_hat = d_part_hat + d_in * single_gain[sublayer]
    single_part_grad = part_norm_back(d_part_hat)[0]
    single_grad = lax.all_gather(single_part_grad, "samp", axis=1, tiled=True)
    grad_cond = jnp.stack(cond_grads)
    part_qkvg, part_out, part_in_w, part_down, part_cond = (
        lax.psum_scatter(
            grad_qkvg.astype(jnp.bfloat16), "blk", scatter_dimension=1, tiled=True
        ).astype(jnp.float32),
        lax.psum_scatter(
            grad_out.astype(jnp.bfloat16), "blk", scatter_dimension=1, tiled=True
        ).astype(jnp.float32),
        lax.psum_scatter(
            grad_in.astype(jnp.bfloat16), "blk", scatter_dimension=1, tiled=True
        ).astype(jnp.float32),
        lax.psum_scatter(
            grad_down.astype(jnp.bfloat16), "blk", scatter_dimension=1, tiled=True
        ).astype(jnp.float32),
        lax.psum_scatter(
            grad_cond.astype(jnp.bfloat16), "blk", scatter_dimension=2, tiled=True
        ).astype(jnp.float32),
    )
    qkvg_grad, out_grad, in_grad, down_grad, cond_grad = (
        lax.psum_scatter(
            part_qkvg.astype(jnp.bfloat16), "samp", scatter_dimension=0, tiled=True
        ).astype(jnp.float32),
        lax.psum_scatter(
            part_out.astype(jnp.bfloat16), "samp", scatter_dimension=0, tiled=True
        ).astype(jnp.float32),
        lax.psum_scatter(
            part_in_w.astype(jnp.bfloat16), "samp", scatter_dimension=0, tiled=True
        ).astype(jnp.float32),
        lax.psum_scatter(
            part_down.astype(jnp.bfloat16), "samp", scatter_dimension=0, tiled=True
        ).astype(jnp.float32),
        lax.psum_scatter(
            part_cond.astype(jnp.bfloat16), "samp", scatter_dimension=1, tiled=True
        ).astype(jnp.float32),
    )
    query_bias_grad, cond_bias_grad, single_gain_grad, pair_gain_grad, pair_weight_grad = lax.psum(
        (
            grad_query_bias,
            jnp.stack(cond_bias_grads),
            jnp.stack(gain_grads),
            grad_pair_gain,
            grad_pair_weight,
        ),
        ("samp", "blk"),
    )
    return (
        block_out,
        act_grad,
        single_grad,
        pair_grad,
        qkvg_grad,
        query_bias_grad,
        out_grad,
        in_grad,
        down_grad,
        cond_grad,
        cond_bias_grad,
        single_gain_grad,
        pair_gain_grad,
        pair_weight_grad,
    )


def solution(mesh):
    return jax.shard_map(
        local,
        mesh=mesh,
        in_specs=(
            P("samp", "blk", None),
            P(None, "blk", None),
            P(None, "blk", "samp", None),
            P("samp"),
            P(),
            P(),
            P(),
            P(),
            P(),
            P(),
            P(),
            P(),
            P(),
            P(),
            P(),
            P("samp", "blk", None),
        ),
        out_specs=(
            P("samp", "blk", None),
            P("samp", "blk", None),
            P(None, "blk", None),
            P(None, "blk", "samp", None),
            P("samp", "blk"),
            P(),
            P("samp", "blk"),
            P("samp", "blk"),
            P("samp", "blk"),
            P(None, "samp", "blk"),
            P(),
            P(),
            P(),
            P(),
        ),
        check_vma=False,
    )
```

profile of v0, /device:TPU:0, one launch (start us, length us, event | category | flops | bytes accessed | tf_op | source)
XLA Modules:
  0.0 1775.3 jit_solution(7725794004818120238)
XLA Ops:
  23.3 7.1 fusion.170
  33.6 24.2 %copy.75 = bf16[2,512,64,128]{1,3,2,0:T(8,128)(2,1)} copy(bf16[2,512,64,128]{3,2,1,0:T(8,128)(2,1)} %param.22) | data formatting | bytes 33554432 | tf_op args[2]
  57.7 7.0 convert_reduce_fusion
  64.8 3.6 copy-done.4
  68.4 4.9 fusion.40
  74.8 6.2 convert_bitcast_fusion
  85.4 4.6 copy.77
  90.1 161.9 %all-gather.6.cloned.1.call-done = bf16[2,512,16,1024]{1,2,3,0:T(8,128)(2,1)} async-done(((bf16[2,512,16,64]{1,2,3,0:T(8,128)(2,1)}), bf16[2,512,16,1024]{1,2,3,0:T(8,128)(2,1)}) %all-gather.6.cloned.1.call-update) | async-done | bytes 33554448 | tf_op jit(solution)/shard_map/all_gather | solution.py:90
  251.9 22.5 %copy.78 = bf16[2,512,16,1024]{1,3,2,0:T(8,128)(2,1)} copy(bf16[2,512,16,1024]{1,2,3,0:T(8,128)(2,1)} %all-gather.6.cloned.1.call-done) | data formatting | bytes 67108864
  274.5 63.6 %while.34 = (s32[]{:T(128)}, f32[1,512,16]{1,2,0:T(8,128)S(1)}, f32[1,512,16]{1,2,0:T(8,128)S(1)}, f32[1,512,16,48]{1,3,2,0:T(8,128)}, s32[2]{0:T(128)S(1)}, /*i...) while((s32[]{:T(128)}, f32[1,512,16]{1,2,0:T(8,128)S(1)}, ...), condition=%wide.region_9.10_spmd.clone, body=%wide.region_6.9_spmd.clone.sunk | while | flops 848479232 | bytes 88868160 | solution.py:143
  277.2 12.0 fusion.219
  289.2 8.4 fusion.221
  297.6 7.3 bitcast_add_fusion.9
  308.8 12.0 fusion.219
  320.8 8.4 fusion.221
  329.2 7.3 bitcast_add_fusion.9
  349.4 4.0 fusion.165
  368.4 3.7 fusion.106
  375.9 10.9 broadcast_in_dim.184
  386.8 127.4 %while.35 = (s32[]{:T(128)}, f32[1,512,16,48]{1,3,2,0:T(8,128)S(1)}, bf16[1,1024,1536]{1,2,0:T(8,128)(2,1)}, bf16[2,512,16,1024]{1,3,2,0:T(8,128)(2,1)}, s32[2]{...) while((s32[]{:T(128)}, ...), condition=%wide.region_16.17_spmd.clone, body=%wide.region_15.16_spmd.clone.sunk | while | flops 2106459136 | bytes 235734480 | solution.py:251
  390.7 13.1 fusion.231
  403.8 9.3 fusion.232
  413.1 14.1 convert_select_fusion.3
  427.2 5.0 bitcast_add_fusion.10
  433.0 4.7 fusion.233
  440.1 10.6 maximum_dynamic-update-slice_fusion.5
  454.4 13.1 fusion.231
  467.4 9.3 fusion.232
  476.8 14.1 convert_select_fusion.3
  490.8 5.0 bitcast_add_fusion.10
  496.6 4.7 fusion.233
  503.7 10.5 maximum_dynamic-update-slice_fusion.5
  518.3 4.7 subtract_multiply_fusion
  525.7 32.0 %reduce-scatter.22.cloned.1.call-done = bf16[1,512,1536]{1,2,0:T(8,128)(2,1)} async-done(((bf16[1,1024,1536]{1,2,0:T(8,128)(2,1)}), bf16[1,512,1536]{1,2,0:T(8,128)(2,1)}) %reduce-scatter.22.cloned.1.call-update) | async-done | bytes 1572880 | tf_op jit(solution)/shard_map/reduce_scatter | solution.py:264
  557.8 6.8 fusion.82
  568.6 4.3 maximum_maximum_fusion
  573.0 3.2 convolution_convert_fusion.3
  578.7 4.9 convolution_convert_fusion.2
  583.5 4.4 copy.99
  588.0 7.4 convolution_convert_fusion
  595.9 7.0 convolution_convert_fusion.1
  603.0 81.5 %reduce-scatter.24.cloned.1.call-done = bf16[2,32,4608]{2,1,0:T(8,128)(2,1)} async-done(((bf16[2,512,4608]{2,1,0:T(8,128)(2,1)}), bf16[2,32,4608]{2,1,0:T(8,128)(2,1)}) %reduce-scatter.24.cloned.1.call-update) | async-done | bytes 589840 | tf_op jit(solution)/shard_map/reduce_scatter | solution.py:290
  689.8 10.5 copy.101
  700.3 4.4 copy.106
  704.8 3.3 reduce-scatter.40.cloned.1.call-done
  710.3 34.7 %reduce-scatter.42.cloned.1.call-done = bf16[384,1536]{1,0:T(8,128)(2,1)} async-done(((bf16[768,1536]{1,0:T(8,128)(2,1)}), bf16[384,1536]{1,0:T(8,128)(2,1)}) %reduce-scatter.42.cloned.1.call-update) | async-done | bytes 1179664
  747.5 59.9 %reduce-scatter.34.cloned.1.call-done = bf16[768,1536]{1,0:T(8,128)(2,1)} async-done(((bf16[768,3072]{1,0:T(8,128)(2,1)}), bf16[768,1536]{1,0:T(8,128)(2,1)}) %reduce-scatter.34.cloned.1.call-update) | async-done | bytes 2359312 | tf_op jit(solution)/shard_map/reduce_scatter | solution.py:337
  807.5 62.4 %reduce-scatter.28.cloned.1.call-done = bf16[768,1536]{1,0:T(8,128)(2,1)} async-done(((bf16[768,3072]{1,0:T(8,128)(2,1)}), bf16[768,1536]{1,0:T(8,128)(2,1)}) %reduce-scatter.28.cloned.1.call-update) | async-done | bytes 2359312 | tf_op jit(solution)/shard_map/reduce_scatter | solution.py:331
  878.0 42.3 %reduce-scatter.44.cloned.1.call-done = bf16[1152,768]{1,0:T(8,128)(2,1)} async-done(((bf16[2304,768]{1,0:T(8,128)(2,1)}), bf16[1152,768]{1,0:T(8,128)(2,1)}) %reduce-scatter.44.cloned.1.call-update) | async-done | bytes 1769488
  920.4 4.5 reshape.780
  924.9 6.8 copy.103
  935.3 44.3 %reduce-scatter.32.cloned.1.call-done = bf16[48,384]{1,0:T(8,128)(2,1)} async-done(((bf16[768,384]{1,0:T(8,128)(2,1)}), bf16[48,384]{1,0:T(8,128)(2,1)}) %reduce-scatter.32.cloned.1.call-update) | async-done | bytes 36880 | tf_op jit(solution)/shard_map/reduce_scatter | solution.py:351
  985.3 55.1 %reduce-scatter.38.cloned.1.call-done = bf16[96,384]{1,0:T(8,128)(2,1)} async-done(((bf16[1536,384]{1,0:T(8,128)(2,1)}), bf16[96,384]{1,0:T(8,128)(2,1)}) %reduce-scatter.38.cloned.1.call-update) | async-done | bytes 73744 | tf_op jit(solution)/shard_map/reduce_scatter | solution.py:357
  1042.0 64.1 %reduce-scatter.36.cloned.1.call-done = bf16[48,1536]{1,0:T(8,128)(2,1)} async-done(((bf16[768,1536]{1,0:T(8,128)(2,1)}), bf16[48,1536]{1,0:T(8,128)(2,1)}) %reduce-scatter.36.cloned.1.call-update) | async-done | bytes 147472 | tf_op jit(solution)/shard_map/reduce_scatter | solution.py:354
  1107.7 64.6 %reduce-scatter.30.cloned.1.call-done = bf16[48,1536]{1,0:T(8,128)(2,1)} async-done(((bf16[768,1536]{1,0:T(8,128)(2,1)}), bf16[48,1536]{1,0:T(8,128)(2,1)}) %reduce-scatter.30.cloned.1.call-update) | async-done | bytes 147472 | tf_op jit(solution)/shard_map/reduce_scatter | solution.py:348
  1174.2 39.5 %all-gather.8.cloned.1.call-done = f32[2,512,384]{2,1,0:T(8,128)} async-done(((f32[2,32,384]{2,1,0:T(8,128)}), f32[2,512,384]{2,1,0:T(8,128)}) %all-gather.8.cloned.1.call-update) | async-done | bytes 1572880 | tf_op jit(solution)/shard_map/all_gather | solution.py:328
  1213.7 63.3 %reduce-scatter.46.cloned.1.call-done = bf16[24,2304]{1,0:T(8,128)(2,1)} async-done(((bf16[384,2304]{1,0:T(8,128)(2,1)}), bf16[24,2304]{1,0:T(8,128)(2,1)}) %reduce-scatter.46.cloned.1.call-update) | async-done | bytes 110608
  1278.7 334.1 %reduce-scatter.26.cloned.1.call-done = bf16[2,512,16,64]{1,3,2,0:T(8,128)(2,1)} async-done(((bf16[2,512,16,1024]{1,3,2,0:T(8,128)(2,1)}), bf16[2,512,16,64]{1,3,2,0:T(8,128)(2,1)}) %reduce-scatter.26.cloned.1.call-update) | async-done | bytes 2097168 | tf_op jit(solution)/shard_map/reduce_scatter | solution.py:287
  1612.7 20.0 %fusion.41 = (f32[2,512,64]{1,2,0:T(8,128)S(1)}, f32[2,512,64,128]{1,3,2,0:T(8,128)}) fusion(bf16[2,512,64,128]{1,3,2,0:T(8,128)(2,1)} %copy.75, f32[128]{0:T(128)S(1)} %copy-done.60, f32[2,512,64]{1,2,0:T(8,128)S(1)} %copy-done.26, bf16[128,16]{0,1:T(8,128)(2,1)S(1)} %copy-done.66, bf16[2,512,16,64]{1,3,2,0:T(8,128)(2,1)} %reduce-scatter.26.cloned.1.call-done), kind=kOutput, calls=%fused_computation.60 | convolution fusion | flops 310312960 | bytes 52957696 | tf_op jit(solution)/shard_map/crhk,zh->crkz/dot_general | solution.py:298
  1632.8 21.4 %fusion.39 = (f32[128]{0:T(128)S(1)}, f32[2,512,64]{1,2,0:T(8,128)S(1)}) fusion(f32[2,512,64,128]{1,3,2,0:T(8,128)} %get-tuple-element.610, bf16[2,512,64,128]{1,3,2,0:T(8,128)(2,1)} %copy.75, f32[2,512,64]{1,2,0:T(8,128)S(1)} %copy-done.31, f32[2,512,64]{1,2,0:T(8,128)S(1)} %copy-done.26, f32[2,512,64]{1,2,0:T(8,128)S(1)} %multiply_multiply_fusion, ...), kind=kLoop, calls=%fused_computation.58 | loop fusion | flops 92209024 | bytes 51381248 | tf_op jit(solution)/shard_map/reduce_sum | solution.py:301
  1654.3 29.2 %broadcast_add_fusion = f32[2,512,64,128]{1,3,2,0:T(8,128)} fusion(f32[2,512,64]{1,2,0:T(8,128)S(1)} %negate_multiply_fusion, f32[2,512,64]{1,2,0:T(8,128)S(1)} %multiply_multiply_fusion, f32[2,512,64]{1,2,0:T(8,128)S(1)} %copy-done.26, bf16[2,512,64,128]{1,3,2,0:T(8,128)(2,1)} %copy.75, f32[2,512,64]{1,2,0:T(8,128)S(1)} %copy-done.31, ...), kind=kLoop, calls=%fused_computation.61 | loop fusion | flops 67108864 | bytes 84935168 | tf_op jit(solution)/shard_map/transpose(jvp())/add_any | solution.py:13
  1683.5 32.2 %copy.88 = f32[2,512,64,128]{3,2,1,0:T(8,128)} copy(f32[2,512,64,128]{1,3,2,0:T(8,128)} %broadcast_add_fusion) | data formatting | bytes 67108864
  1715.7 10.6 fusion.117
  1726.3 39.7 %all-reduce.1 = (f32[768]{0:T(1024)}, f32[2,1536]{1,0:T(2,128)}, f32[2,384]{1,0:T(2,128)}, f32[128]{0:T(128)}, f32[128,16]{0,1:T(8,128)}) all-reduce(f32[768]{0:T(1024)S(1)} %reshape.756, f32[2,1536]{1,0:T(2,128)S(1)} %pad_maximum_fusion.13, f32[2,384]{1,0:T(2,128)S(1)} %pad_maximum_fusion.16, ...), channel_id=1, replica_groups=mesh['samp'=16,'blk'=2] {'samp','blk'}, use_global_device_ids=true, to_apply=%region_31.32 | all-reduce | flops 6784 | bytes 54272 | tf_op jit(solution)/shard_map/psum | solution.py:364
  (325 shorter events, 121.9 us)
Async XLA Ops:
  7.2 349.9 %copy-start = (bf16[1536,768]{1,0:T(8,128)(2,1)S(1)}, bf16[1536,768]{1,0:T(8,128)(2,1)}, u32[]{:S(2)}) copy-start(bf16[1536,768]{1,0:T(8,128)(2,1)} %param.29) | copy-start | bytes 7077892
  7.2 4.4 copy-start.24
  7.2 5.1 copy-start.68
  7.2 5.1 copy-start.58
  7.2 5.2 copy-start.67
  7.2 78.2 %all-gather.4.cloned.1.call-start = ((), (), s32[]{:S(2)}) async-start(), calls=%async_computation.13 | async-start | bytes 4718592 | tf_op jit(solution)/shard_map/all_gather | solution.py:155
  9.5 11.6 copy-start.46
  11.6 9.5 copy-start.50
  23.3 7.1 copy-start.43
  33.3 218.6 %all-gather.6.cloned.1.call-start = ((), (), s32[]{:S(2)}) async-start(), calls=%async_computation.14 | async-start | bytes 35651584 | tf_op jit(solution)/shard_map/all_gather | solution.py:90
  57.7 10.7 copy-start.4
  68.4 5.7 copy-start.25
  68.4 6.4 copy-start.59
  68.4 6.4 copy-start.65
  81.1 476.7 %reduce-scatter.22.cloned.1.call-start = ((), (), s32[]{:S(2)}) async-start(), calls=%async_computation.15 | async-start | bytes 4718592 | tf_op jit(solution)/shard_map/reduce_scatter | solution.py:264
  289.2 8.4 copy-start.9
  320.8 8.4 copy-start.9
  343.8 10.6 slice-start.4
  346.9 6.9 slice-start.2
  349.4 4.4 slice-start.3
  349.4 5.0 slice-start.5
  353.5 9.3 copy-start.16
  353.5 9.3 copy-start.48
  353.8 9.0 copy-start.54
  375.9 10.9 copy-start.5
  387.0 26.1 %copy-start.6 = (bf16[1,512,16,48]{1,3,2,0:T(8,128)(2,1)}, bf16[1,512,16,48]{1,3,2,0:T(8,128)(2,1)S(1)}, u32[]{:S(2)}) copy-start(bf16[1,512,16,48]{1,3,2,0:T(8,128)(2,1)S(1)} %get-tuple-element.880) | copy-start | bytes 2359300 | tf_op jit(solution)/shard_map/while
  427.2 5.8 copy-start.2
  433.0 4.7 copy-start.8
  433.0 7.1 copy-start.3
  440.1 10.6 copy-start.7
  450.7 26.1 %copy-start.6 = (bf16[1,512,16,48]{1,3,2,0:T(8,128)(2,1)}, bf16[1,512,16,48]{1,3,2,0:T(8,128)(2,1)S(1)}, u32[]{:S(2)}) copy-start(bf16[1,512,16,48]{1,3,2,0:T(8,128)(2,1)S(1)} %get-tuple-element.880) | copy-start | bytes 2359300 | tf_op jit(solution)/shard_map/while
  490.8 5.8 copy-start.2
  496.6 4.7 copy-start.8
  496.6 7.1 copy-start.3
  503.7 10.5 copy-start.7
  514.3 170.2 %reduce-scatter.24.cloned.1.call-start = ((), (), s32[]{:S(2)}) async-start(), calls=%async_computation.16 | async-start | bytes 10027008 | tf_op jit(solution)/shard_map/reduce_scatter | solution.py:290
  523.0 34.8 %copy-start.15 = (bf16[1,512,768]{2,1,0:T(8,128)(2,1)S(1)}, bf16[1,512,768]{2,1,0:T(8,128)(2,1)}, u32[]{:S(2)}) copy-start(bf16[1,512,768]{2,1,0:T(8,128)(2,1)} %param.20) | copy-start | bytes 2359300
  523.0 34.8 %copy-start.47 = (f32[512]{0:T(512)S(1)}, f32[512]{0:T(512)}, u32[]{:S(2)}) copy-start(f32[512]{0:T(512)} %copy-done.46) | copy-start | bytes 6148
  557.8 6.9 slice-start
  557.8 6.9 slice-start.1
  557.8 6.9 copy-start.18
  557.8 6.9 copy-start.39
  557.8 6.9 copy-start.51
  557.8 6.9 copy-start.53
  572.9 135.2 %reduce-scatter.40.cloned.1.call-start = ((), (), s32[]{:S(2)}) async-start(), calls=%async_computation.25 | async-start | bytes 1769472
  578.6 166.4 %reduce-scatter.42.cloned.1.call-start = ((), (), s32[]{:S(2)}) async-start(), calls=%async_computation.26 | async-start | bytes 3538944
  588.0 219.4 %reduce-scatter.34.cloned.1.call-start = ((), (), s32[]{:S(2)}) async-start(), calls=%async_computation.22 | async-start | bytes 7077888 | tf_op jit(solution)/shard_map/reduce_scatter | solution.py:337
  595.5 274.4 %reduce-scatter.28.cloned.1.call-start = ((), (), s32[]{:S(2)}) async-start(), calls=%async_computation.19 | async-start | bytes 7077888 | tf_op jit(solution)/shard_map/reduce_scatter | solution.py:331
  602.9 317.5 %reduce-scatter.44.cloned.1.call-start = ((), (), s32[]{:S(2)}) async-start(), calls=%async_computation.27 | async-start | bytes 5308416
  704.8 274.9 %reduce-scatter.32.cloned.1.call-start = ((), (), s32[]{:S(2)}) async-start(), calls=%async_computation.21 | async-start | bytes 626688 | tf_op jit(solution)/shard_map/reduce_scatter | solution.py:351
  710.3 330.2 %reduce-scatter.38.cloned.1.call-start = ((), (), s32[]{:S(2)}) async-start(), calls=%async_computation.24 | async-start | bytes 1253376 | tf_op jit(solution)/shard_map/reduce_scatter | solution.py:357
  747.5 358.6 %reduce-scatter.36.cloned.1.call-start = ((), (), s32[]{:S(2)}) async-start(), calls=%async_computation.23 | async-start | bytes 2506752 | tf_op jit(solution)/shard_map/reduce_scatter | solution.py:354
  807.4 364.9 %reduce-scatter.30.cloned.1.call-start = ((), (), s32[]{:S(2)}) async-start(), calls=%async_computation.20 | async-start | bytes 2506752 | tf_op jit(solution)/shard_map/reduce_scatter | solution.py:348
  869.8 343.9 %all-gather.8.cloned.1.call-start = ((), (), s32[]{:S(2)}) async-start(), calls=%async_computation.17 | async-start | bytes 1671168 | tf_op jit(solution)/shard_map/all_gather | solution.py:328
  878.0 399.0 %reduce-scatter.46.cloned.1.call-start = ((), (), s32[]{:S(2)}) async-start(), calls=%async_computation.28 | async-start | bytes 1880064
  934.6 678.1 %reduce-scatter.26.cloned.1.call-start = ((), (), s32[]{:S(2)}) async-start(), calls=%async_computation.18 | async-start | bytes 35651584 | tf_op jit(solution)/shard_map/reduce_scatter | solution.py:287
  934.7 46.4 %copy-start.57 = (f32[512]{0:T(512)S(1)}, f32[512]{0:T(512)}, u32[]{:S(2)}) copy-start(f32[512]{0:T(512)} %copy-done.56) | copy-start | bytes 6148
  983.8 190.2 %copy-start.36 = (bf16[2,32,4608]{2,1,0:T(8,128)(2,1)S(1)}, bf16[2,32,4608]{2,1,0:T(8,128)(2,1)}, u32[]{:S(2)}) copy-start(bf16[2,32,4608]{2,1,0:T(8,128)(2,1)} %reduce-scatter.24.cloned.1.call-done) | copy-start | bytes 1769476
  985.3 627.5 %copy-start.26 = (f32[2,512,64]{1,2,0:T(8,128)S(1)}, f32[2,512,64]{1,2,0:T(8,128)}, u32[]{:S(2)}) copy-start(f32[2,512,64]{1,2,0:T(8,128)} %copy-done.25) | copy-start | bytes 786436
  985.3 627.5 %copy-start.60 = (f32[128]{0:T(128)S(1)}, f32[128]{0:T(128)}, u32[]{:S(2)}) copy-start(f32[128]{0:T(128)} %param.33) | copy-start | bytes 1540
  985.3 627.5 %copy-start.66 = (bf16[128,16]{0,1:T(8,128)(2,1)S(1)}, bf16[128,16]{0,1:T(8,128)(2,1)}, u32[]{:S(2)}) copy-start(bf16[128,16]{0,1:T(8,128)(2,1)} %param.34) | copy-start | bytes 12292
  1278.7 354.1 %copy-start.33 = (f32[2,512,64]{1,2,0:T(8,128)S(1)}, f32[2,512,64]{1,2,0:T(8,128)}, u32[]{:S(2)}) copy-start(f32[2,512,64]{1,2,0:T(8,128)} %copy-done.32) | copy-start | bytes 786436
  1278.7 354.2 %copy-start.31 = (f32[2,512,64]{1,2,0:T(8,128)S(1)}, f32[2,512,64]{1,2,0:T(8,128)}, u32[]{:S(2)}) copy-start(f32[2,512,64]{1,2,0:T(8,128)} %copy-done.30) | copy-start | bytes 786436
  1715.7 52.9 %copy-start.1 = (bf16[1536,768]{1,0:T(8,128)(2,1)S(1)}, bf16[1536,768]{1,0:T(8,128)(2,1)}, u32[]{:S(2)}) copy-start(bf16[1536,768]{1,0:T(8,128)(2,1)} %param.29) | copy-start | bytes 7077892
  (40 other events, 96.9 us)
Sparse Core Ops, SparseCore 0:
  33.4 47.6 all-gather.3
  82.7 169.2 all-gather.5
  514.4 43.3 reduce-scatter.21
  573.1 111.3 reduce-scatter.23
  686.6 21.4 reduce-scatter.39
  710.3 34.6 reduce-scatter.41
  747.3 59.9 reduce-scatter.33
  809.8 59.9 reduce-scatter.27
  872.6 47.6 reduce-scatter.43
  924.8 54.8 reduce-scatter.31
  983.2 57.1 reduce-scatter.37
  1044.0 61.9 reduce-scatter.35
  1110.3 61.9 reduce-scatter.29
  1175.0 38.6 all-gather.7
  1217.9 59.0 reduce-scatter.45
  1281.1 331.5 reduce-scatter.25
where the time goes:
time: 1790 us; the launch traced here: 1780 us
  waiting for transfers between devices  1140 us (64%)
  matrix products  236 us (13%)
  local copies, waits for them, and re-layouts  180 us (10%)
  other arithmetic  154 us (9%)
  blocking collectives  39.7 us (2%)
    reduce_scatter x1, waiting for transfers between devices, local(): lax.psum_scatter(d_bias.astype(jnp.bfloat16), 'samp', scatter_dimension=3...  334 us
    all_gather x1, waiting for transfers between devices, local(): bias_all = lax.all_gather(bias_local, 'samp', axis=3, tiled=True)  162 us
    unnamed x20, waiting for transfers between devices  144 us
    unnamed x163, local copies, waits for them, and re-layouts  142 us
    reduce_scatter x1, waiting for transfers between devices, local(): lax.psum_scatter(d_cond_all.astype(jnp.bfloat16), 'samp', scatter_dimensi...  81.5 us
    reduce_scatter x1, waiting for transfers between devices, local(): lax.psum_scatter(part_qkvg.astype(jnp.bfloat16), 'samp', scatter_dimensio...  64.6 us
    reduce_scatter x1, waiting for transfers between devices, local(): lax.psum_scatter(part_in_w.astype(jnp.bfloat16), 'samp', scatter_dimensio...  64.1 us
    reduce_scatter x1, waiting for transfers between devices, local(): lax.psum_scatter(grad_qkvg.astype(jnp.bfloat16), 'blk', scatter_dimension...  62.4 us
  transfers between devices with their start and end apart: 16, of which 15 were waited for; matrix products, arithmetic and copies ran while one was open for 8% of the time, Pallas kernels for 0%

commit v1 on v0

--- a/solution.py
+++ b/solution.py
@@ -1,12 +1,19 @@
+import functools
 import math
 
 import jax
 import jax.numpy as jnp
 from jax import lax
+from jax.experimental import pallas as pl
+from jax.experimental.pallas import tpu as pltpu
 from jax.sharding import PartitionSpec as P
 
 EPS = 1e-05
 MASKED = -1000000000.0
+LOG2E = 1.4426950408889634
+LN2 = 0.6931471805599453
+VMEM_BYTES = 56 * 1024 * 1024
+TILE_COLS = 384
 
 
 def norm_rows(value):
@@ -389,9 +396,993 @@
     )
 
 
+FORWARD_GROUP = 4
+BACKWARD_GROUP = 4
+KEY_CHUNK = 128
+
+
+def nt_dot(left, right):
+    return lax.dot_general(
+        left, right, (((1,), (1,)), ((), ())), preferred_element_type=jnp.float32
+    )
+
+
+def nn_dot(left, right):
+    return lax.dot_general(
+        left, right, (((1,), (0,)), ((), ())), preferred_element_type=jnp.float32
+    )
+
+
+def tn_dot(left, right):
+    return lax.dot_general(
+        left, right, (((0,), (0,)), ((), ())), preferred_element_type=jnp.float32
+    )
+
+
+def split_two(value):
+    high = value.astype(jnp.bfloat16)
+    return high, (value - high.astype(jnp.float32)).astype(jnp.bfloat16)
+
+
+def spends(micros):
+    return pl.CostEstimate(
+        flops=int(micros * 1e9), bytes_accessed=int(micros * 3e6), transcendentals=0
+    )
+
+
+def pair_rows(pair_ref):
+    quarters, rows, cols, chans = pair_ref.shape[2:]
+    both = jnp.concatenate([pair_ref[0, 0, quarter] for quarter in range(quarters)], axis=1)
+    return both.reshape(rows * quarters * cols, chans)
+
+
+def pair_forward_kernel(pair_ref, coef_ref, coef_sum_ref, bias_ref, mean_ref, rstd_ref):
+    heads = bias_ref.shape[0]
+    rows, lanes = mean_ref.shape[2:]
+    chans = pair_ref.shape[5]
+    cells = pair_rows(pair_ref)
+    wide = cells.astype(jnp.float32)
+    square_high, square_low = split_two(wide * wide)
+    sums = nt_dot(coef_ref[...], jnp.concatenate([cells, square_high], axis=1))
+    low_sums = nt_dot(jnp.ones((16, chans), jnp.bfloat16), square_low)
+    raw = sums[:heads] + sums[heads : 2 * heads]
+    total = sums[2 * heads : 2 * heads + 1]
+    squares = sums[2 * heads + 8 : 2 * heads + 9] + low_sums[0:1]
+    total_high = total.astype(jnp.bfloat16).astype(jnp.float32)
+    total_low = total - total_high
+    spread = squares * chans - total_high * total_high
+    spread = spread - 2.0 * total_high * total_low - total_low * total_low
+    rstd = lax.rsqrt(jnp.maximum(spread, 0.0) * (1.0 / (chans * chans)) + EPS)
+    mean = total * (1.0 / chans)
+    bias = (raw - coef_sum_ref[...] * mean) * (rstd * LOG2E)
+    bias_ref[:, 0, 0] = bias.reshape(heads, rows, lanes).astype(jnp.bfloat16)
+    mean_ref[0, 0] = mean.reshape(rows, lanes)
+    rstd_ref[0, 0] = rstd.reshape(rows, lanes)
+
+
+def pair_forward(pair, pair_gain, pair_weight):
+    structs, halves, quarters, rows, cols, chans = pair.shape
+    heads = pair_weight.shape[1]
+    lanes = quarters * cols
+    step = 32
+    gained = pair_weight.astype(jnp.float32) * pair_gain[:, None]
+    high, low = split_two(gained.T)
+    ones_row = jnp.zeros((8, chans), jnp.bfloat16).at[0].set(1.0)
+    blank = jnp.zeros((8, chans), jnp.bfloat16)
+    coef = jnp.concatenate(
+        [
+            jnp.concatenate([high, low, ones_row, blank], axis=0),
+            jnp.concatenate([jnp.zeros((2 * heads, chans), jnp.bfloat16), blank, ones_row], axis=0),
+        ],
+        axis=1,
+    )
+    coef_sum = jnp.sum(gained, axis=0)[:, None]
+    return pl.pallas_call(
+        pair_forward_kernel,
+        grid=(halves, structs, rows // step),
+        in_specs=[
+            pl.BlockSpec((1, 1, quarters, step, cols, chans), lambda h, c, r: (c, h, 0, r, 0, 0)),
+            pl.BlockSpec(coef.shape, lambda h, c, r: (0, 0)),
+            pl.BlockSpec(coef_sum.shape, lambda h, c, r: (0, 0)),
+        ],
+        out_specs=[
+            pl.BlockSpec((heads, 1, 1, step, lanes), lambda h, c, r: (0, h, c, r, 0)),
+            pl.BlockSpec((1, 1, step, lanes), lambda h, c, r: (h, c, r, 0)),
+            pl.BlockSpec((1, 1, step, lanes), lambda h, c, r: (h, c, r, 0)),
+        ],
+        out_shape=[
+            jax.ShapeDtypeStruct((heads, halves, structs, rows, lanes), jnp.bfloat16),
+            jax.ShapeDtypeStruct((halves, structs, rows, lanes), jnp.float32),
+            jax.ShapeDtypeStruct((halves, structs, rows, lanes), jnp.float32),
+        ],
+        compiler_params=pltpu.CompilerParams(vmem_limit_bytes=VMEM_BYTES),
+        cost_estimate=spends(20),
+        name="pair_forward",
+    )(pair, coef, coef_sum)
+
+
+def pair_backward_kernel(
+    pair_ref, d_bias_ref, bias_ref, mean_ref, rstd_ref, coef_ref, coef_sum_ref, *refs
+):
+    grad_ref, inner_ref, offset_ref = refs[-3:]
+    heads = d_bias_ref.shape[0]
+    rows, lanes = mean_ref.shape[2:]
+    quarters, _, cols, chans = pair_ref.shape[2:]
+    count = rows * lanes
+    cells = pair_rows(pair_ref)
+    d_bias = d_bias_ref[:, 0, 0].astype(jnp.float32)
+    bias = bias_ref[:, 0, 0].astype(jnp.float32)
+    mean = mean_ref[0]
+    rstd = rstd_ref[0]
+    g_mean = jnp.sum(d_bias * coef_sum_ref[...], axis=0, keepdims=True) * (1.0 / chans)
+    gy_mean = jnp.sum(d_bias * bias, axis=0, keepdims=True) * (LN2 / chans)
+    slope = rstd * rstd * gy_mean
+    shift = mean * slope - rstd * g_mean
+    scaled = d_bias * rstd
+
+    @pl.when((pl.program_id(0) == 0) & (pl.program_id(1) == 0))
+    def _():
+        inner_ref[...] = jnp.zeros_like(inner_ref)
+        offset_ref[...] = jnp.zeros_like(offset_ref)
+
+    offset_ref[...] += jnp.sum(scaled * mean, axis=1)
+    scaled_high, scaled_low = split_two(scaled.reshape(heads, count))
+    ends = jnp.concatenate([shift, slope], axis=0).reshape(2, count)
+    ends_high, ends_low = split_two(ends)
+    blank = jnp.zeros((12, count), jnp.bfloat16)
+    inner_ref[...] += nn_dot(jnp.concatenate([scaled_high, scaled_low], axis=0), cells)
+    factors = jnp.concatenate([scaled_high, scaled_low, ends_high, ends_low, blank], axis=0)
+    spread = tn_dot(factors, coef_ref[...])
+    grad = spread[:, :chans] - cells.astype(jnp.float32) * spread[:, chans:]
+    grad = grad.reshape(rows, lanes, chans)
+    for quarter in range(quarters):
+        grad_ref[0, 0, quarter] = grad[:, quarter * cols : (quarter + 1) * cols]
+
+
+def pair_backward(half, pair, d_bias, bias, mean, rstd, pair_gain, pair_weight, partial):
+    structs, _, quarters, half_rows, cols, chans = pair.shape
+    heads = pair_weight.shape[1]
+    lanes = quarters * cols
+    step = 32
+    gained = (pair_weight.astype(jnp.float32) * pair_gain[:, None]).T
+    coef_sum = jnp.sum(gained, axis=1)[:, None, None]
+    ones = jnp.ones((1, chans), jnp.bfloat16)
+    zeros = jnp.zeros((1, chans), jnp.bfloat16)
+    rows = gained.astype(jnp.bfloat16)
+    left = jnp.concatenate([rows, rows, ones, zeros, ones, zeros], axis=0)
+    right = jnp.concatenate(
+        [jnp.zeros((2 * heads, chans), jnp.bfloat16), zeros, ones, zeros, ones], axis=0
+    )
+    coef = jnp.concatenate([left, right], axis=1)
+    coef = jnp.concatenate([coef, jnp.zeros((12, 2 * chans), jnp.bfloat16)], axis=0)
+    grad, inner, offset = pl.pallas_call(
+        pair_backward_kernel,
+        grid=(structs, half_rows // step),
+        in_specs=[
+            pl.BlockSpec((1, 1, quarters, step, cols, chans), lambda c, r: (c, half, 0, r, 0, 0)),
+            pl.BlockSpec((heads, 1, 1, step, lanes), lambda c, r: (0, half, c, r, 0)),
+            pl.BlockSpec((heads, 1, 1, step, lanes), lambda c, r: (0, half, c, r, 0)),
+            pl.BlockSpec((1, 1, step, lanes), lambda c, r: (half, c, r, 0)),
+            pl.BlockSpec((1, 1, step, lanes), lambda c, r: (half, c, r, 0)),
+            pl.BlockSpec(coef.shape, lambda c, r: (0, 0)),
+            pl.BlockSpec(coef_sum.shape, lambda c, r: (0, 0, 0)),
+        ]
+        + [pl.BlockSpec(memory_space=pl.ANY)] * len(partial),
+        out_specs=[
+            pl.BlockSpec((1, 1, quarters, step, cols, chans), lambda c, r: (c, half, 0, r, 0, 0)),
+            pl.BlockSpec((2 * heads, chans), lambda c, r: (0, 0)),
+            pl.BlockSpec((heads, lanes), lambda c, r: (0, 0)),
+        ],
+        input_output_aliases={7: 0} if partial else {},
+        out_shape=[
+            jax.ShapeDtypeStruct(pair.shape, jnp.float32),
+            jax.ShapeDtypeStruct((2 * heads, chans), jnp.float32),
+            jax.ShapeDtypeStruct((heads, lanes), jnp.float32),
+        ],
+        compiler_params=pltpu.CompilerParams(vmem_limit_bytes=VMEM_BYTES),
+        cost_estimate=spends(13),
+        name="pair_backward",
+    )(pair, d_bias, bias, mean, rstd, coef, coef_sum, *partial)
+    moment = inner[:heads] + inner[heads:] - jnp.sum(offset, axis=1, keepdims=True)
+    grad_weight = moment.T * pair_gain[:, None]
+    grad_gain = jnp.sum(moment.T * pair_weight.astype(jnp.float32), axis=1)
+    return grad, grad_weight, grad_gain
+
+
+def attention_forward_kernel(
+    ids_ref, limits_ref, blk_ref,
+    query_ref, key_own_ref, key_far_ref, value_own_ref, value_far_ref, bias_ref,
+    sent_ref, attn_ref, inverse_ref, weights_ref,
+    table_ref,
+):
+    sources, _, structs, _, lanes = bias_ref.shape
+    tile = query_ref.shape[2]
+    cols = lanes // 2
+    sample = pl.program_id(0)
+    near = sources // 2
+
+    @pl.when(sample == 0)
+    def _():
+        for struct in range(structs):
+            limit = limits_ref[struct]
+            for source in range(sources):
+                part = bias_ref[source, 0, struct].astype(jnp.float32).T
+                part = jnp.concatenate([part[:cols], part[cols:]], axis=1)
+                position = (
+                    lax.rem(source // near + blk_ref[0], 2) * (near * cols) + (source % near) * cols
+                )
+                position = pl.multiple_of(position, cols)
+                keys = source * cols + lax.broadcasted_iota(jnp.int32, part.shape, 0)
+                table_ref[struct, pl.ds(position, cols)] = jnp.where(
+                    keys < limit, part, -1e30
+                ).astype(jnp.bfloat16)
+
+    head_dim = query_ref.shape[1]
+    for member in range(query_ref.shape[0]):
+        struct = ids_ref[sample * query_ref.shape[0] + member]
+        keys_t = jnp.concatenate([key_own_ref[member], key_far_ref[member]], axis=1)
+        keys = keys_t.astype(jnp.float32).T.astype(jnp.bfloat16)
+        values_t = jnp.concatenate([value_own_ref[member], value_far_ref[member]], axis=1)
+        values_t = jnp.concatenate(
+            [values_t, jnp.ones((16, values_t.shape[1]), jnp.bfloat16)], axis=0
+        )
+        query = query_ref[member]
+        scores = []
+        peak = None
+        for start in range(0, keys.shape[0], KEY_CHUNK):
+            part = nn_dot(keys[start : start + KEY_CHUNK], query)
+            part = part + table_ref[struct, start : start + KEY_CHUNK].astype(jnp.float32)
+            part_peak = jnp.max(part.reshape(-1, 8, tile), axis=0)
+            peak = part_peak if peak is None else jnp.maximum(peak, part_peak)
+            scores.append(part)
+        peak = jnp.max(peak, axis=0, keepdims=True)
+        summed = 0.0
+        for index, part in enumerate(scores):
+            span = slice(index * KEY_CHUNK, (index + 1) * KEY_CHUNK)
+            weights = jnp.exp2(part - peak).astype(jnp.bfloat16)
+            weights_ref[member, span] = weights
+            summed = summed + nn_dot(values_t[:, span], weights)
+        inverse = 1.0 / summed[head_dim : head_dim + 1]
+        attn = summed[:head_dim] * inverse
+        attn_ref[member] = attn
+        sent_ref[member] = attn.astype(jnp.bfloat16)
+        inverse_ref[member] = inverse
+
+
+def attention_forward(half, ids, limits, blk, qkv, kv_far, bias):
+    samples, triple, tokens = qkv.shape
+    head_dim = triple // 3
+    structs = bias.shape[2]
+    tile = tokens // 2
+    keys = 2 * tokens
+    group = FORWARD_GROUP
+    part = (group, head_dim, tokens)
+    tile_part = (group, head_dim, tile)
+    grid_spec = pltpu.PrefetchScalarGridSpec(
+        num_scalar_prefetch=3,
+        grid=(samples // group,),
+        in_specs=[
+            pl.BlockSpec(tile_part, lambda n, *_: (n, 0, half)),
+            pl.BlockSpec(part, lambda n, *_: (n, 1, 0)),
+            pl.BlockSpec(part, lambda n, *_: (n, 0, 0)),
+            pl.BlockSpec(part, lambda n, *_: (n, 2, 0)),
+            pl.BlockSpec(part, lambda n, *_: (n, 1, 0)),
+            pl.BlockSpec(
+                (bias.shape[0], 1) + bias.shape[2:], lambda n, *_: (0, half, 0, 0, 0)
+            ),
+        ],
+        out_specs=[
+            pl.BlockSpec(tile_part, lambda n, *_: (n, 0, 0)),
+            pl.BlockSpec(tile_part, lambda n, *_: (n, 0, 0)),
+            pl.BlockSpec((group, 1, tile), lambda n, *_: (n, 0, 0)),
+            pl.BlockSpec((group, keys, tile), lambda n, *_: (n, 0, 0)),
+        ],
+        scratch_shapes=[pltpu.VMEM((structs, keys, tile), jnp.bfloat16)],
+    )
+    return pl.pallas_call(
+        attention_forward_kernel,
+        grid_spec=grid_spec,
+        out_shape=[
+            jax.ShapeDtypeStruct((samples, head_dim, tile), jnp.bfloat16),
+            jax.ShapeDtypeStruct((samples, head_dim, tile), jnp.float32),
+            jax.ShapeDtypeStruct((samples, 1, tile), jnp.float32),
+            jax.ShapeDtypeStruct((samples, keys, tile), jnp.bfloat16),
+        ],
+        compiler_params=pltpu.CompilerParams(vmem_limit_bytes=VMEM_BYTES),
+        cost_estimate=spends(14),
+        name="attention_forward",
+    )(ids, limits, blk, qkv, qkv, kv_far, qkv, kv_far, bias)
+
+
+def attention_backward_kernel(
+    ids_ref, blk_ref,
+    query_ref, key_own_ref, key_far_ref, value_own_ref, value_far_ref,
+    d_attn_ref, attn_ref, inverse_ref, weights_ref, *refs, score_scale,
+):
+    d_query_ref, d_own_ref, d_far_ref, d_bias_ref, total_ref = refs[-5:]
+    sources, structs, _, lanes = d_bias_ref.shape
+    cols = lanes // 2
+    sample = pl.program_id(0)
+    near = sources // 2
+    group, head_dim, tile = query_ref.shape
+    tokens = key_own_ref.shape[2]
+
+    @pl.when(sample == 0)
+    def _():
+        total_ref[...] = jnp.zeros_like(total_ref)
+
+    tail = jnp.zeros((14, tile), jnp.bfloat16)
+    for index in range(group):
+        struct = ids_ref[sample * group + index]
+        keys_t = jnp.concatenate([key_own_ref[index], key_far_ref[index]], axis=1)
+        values_t = jnp.concatenate([value_own_ref[index], value_far_ref[index]], axis=1)
+        values_t = jnp.concatenate(
+            [values_t, jnp.ones((16, values_t.shape[1]), jnp.bfloat16)], axis=0
+        )
+        values = turned(values_t)
+        inverse = inverse_ref[index]
+        d_attn = d_attn_ref[index].astype(jnp.float32)
+        delta = jnp.sum(d_attn * attn_ref[index], axis=0, keepdims=True)
+        d_attn = (d_attn * inverse).astype(jnp.bfloat16)
+        delta_high, delta_low = split_two(-delta * inverse)
+        d_probs = nn_dot(values, jnp.concatenate([d_attn, delta_high, delta_low, tail], axis=0))
+        weights = weights_ref[index]
+        d_scores = weights.astype(jnp.float32) * d_probs
+        total_ref[struct] += d_scores
+        d_scores = d_scores.astype(jnp.bfloat16)
+        d_values = nn_dot(weights, turned(d_attn)).T
+        d_keys = nn_dot(d_scores, turned(query_ref[index])).T * LN2
+        d_query_ref[index] = (nn_dot(keys_t, d_scores) * score_scale).astype(jnp.bfloat16)
+        for place, value in ((slice(0, head_dim), d_keys), (slice(head_dim, None), d_values)):
+            own, far = value[:, :tokens], value[:, tokens:]
+            if len(refs) > 5:
+                own = own + refs[0][index, place].astype(jnp.float32)
+                far = far + refs[1][index, place].astype(jnp.float32)
+            d_own_ref[index, place] = own.astype(jnp.bfloat16)
+            d_far_ref[index, place] = far.astype(jnp.bfloat16)
+
+    @pl.when(sample == pl.num_programs(0) - 1)
+    def _():
+        for member in range(structs):
+            for source in range(sources):
+                position = (
+                    lax.rem(source // near + blk_ref[0], 2) * (near * cols) + (source % near) * cols
+                )
+                position = pl.multiple_of(position, cols)
+                part = total_ref[member, pl.ds(position, cols)]
+                part = jnp.concatenate([part[:, : tile // 2], part[:, tile // 2 :]], axis=0)
+                d_bias_ref[source, member] = part.T.astype(jnp.bfloat16)
+
+
+def attention_backward(half, ids, blk, qkv, kv_far, d_attn, attn, inverse, weights, bias, partial):
+    samples, triple, tokens = qkv.shape
+    head_dim = triple // 3
+    keys, tile = weights.shape[1:]
+    bias_shape = bias.shape[:1] + bias.shape[2:]
+    structs = bias.shape[2]
+    group = BACKWARD_GROUP
+    part = (group, head_dim, tokens)
+    tile_part = pl.BlockSpec((group, head_dim, tile), lambda n, *_: (n, 0, 0))
+    pair_part = pl.BlockSpec((group, 2 * head_dim, tokens), lambda n, *_: (n, 0, 0))
+    grid_spec = pltpu.PrefetchScalarGridSpec(
+        num_scalar_prefetch=2,
+        grid=(samples // group,),
+        in_specs=[
+            pl.BlockSpec((group, head_dim, tile), lambda n, *_: (n, 0, half)),
+            pl.BlockSpec(part, lambda n, *_: (n, 1, 0)),
+            pl.BlockSpec(part, lambda n, *_: (n, 0, 0)),
+            pl.BlockSpec(part, lambda n, *_: (n, 2, 0)),
+            pl.BlockSpec(part, lambda n, *_: (n, 1, 0)),
+            tile_part,
+            tile_part,
+            pl.BlockSpec((group, 1, tile), lambda n, *_: (n, 0, 0)),
+            pl.BlockSpec((group, keys, tile), lambda n, *_: (n, 0, 0)),
+        ]
+        + [pair_part] * len(partial),
+        out_specs=[
+            tile_part, pair_part, pair_part, pl.BlockSpec(bias_shape, lambda n, *_: (0, 0, 0, 0))
+        ],
+        scratch_shapes=[pltpu.VMEM((structs, keys, tile), jnp.float32)],
+    )
+    pair_shape = jax.ShapeDtypeStruct((samples, 2 * head_dim, tokens), jnp.bfloat16)
+    return pl.pallas_call(
+        functools.partial(attention_backward_kernel, score_scale=1.0 / math.sqrt(head_dim)),
+        grid_spec=grid_spec,
+        out_shape=[
+            jax.ShapeDtypeStruct((samples, head_dim, tile), jnp.bfloat16),
+            pair_shape,
+            pair_shape,
+            jax.ShapeDtypeStruct(bias_shape, jnp.bfloat16),
+        ],
+        compiler_params=pltpu.CompilerParams(vmem_limit_bytes=VMEM_BYTES),
+        cost_estimate=spends(13),
+        name="attention_backward",
+    )(ids, blk, qkv, qkv, kv_far, qkv, kv_far, d_attn, attn, inverse, weights, *partial)
+
+
+def turned(value):
+    return value.astype(jnp.float32).T.astype(jnp.bfloat16)
+
+
+def store_tiles(out_refs, core, grad, start):
+    groups = out_refs[0].shape[0]
+    if core is None:
+        rows = grad.reshape(groups, -1, grad.shape[1]).astype(jnp.bfloat16)
+        out_refs[0][:, start : start + rows.shape[1]] = rows
+        return
+    rows = grad.reshape(groups, 2, -1, grad.shape[1]).astype(jnp.bfloat16)
+    span = slice(start, start + rows.shape[2])
+    for mine in range(2):
+
+        @pl.when(core == mine)
+        def _():
+            out_refs[0][:, span] = rows[:, mine]
+            out_refs[1][:, span] = rows[:, 1 - mine]
+
+
+def cond_tiles(out_refs, core, cond_t, d_cond_ref, place, stride):
+    tiles = out_refs[0].shape[0] * (1 if core is None else 2)
+    rows = cond_t.shape[0] // tiles
+    per_blk = d_cond_ref.shape[1] // (2 * TILE_COLS)
+    blank = jnp.zeros((tiles, -(per_blk * rows) % 16, TILE_COLS), jnp.float32)
+    for blk in range(2):
+        parts = []
+        for chunk in range(per_blk):
+            start = (blk * per_blk + chunk) * TILE_COLS
+            grad = nn_dot(cond_t, d_cond_ref[:, start : start + TILE_COLS])
+            parts.append(grad.reshape(tiles, rows, TILE_COLS))
+        grad = jnp.concatenate(parts + [blank], axis=1).reshape(-1, TILE_COLS)
+        store_tiles(out_refs, core, grad, blk * stride + place)
+
+
+def early_grads_kernel(*refs):
+    out_refs = refs[-1:]
+    pairs = [refs[2 * index : 2 * index + 2] for index in range(7)]
+    x_refs, d_up_refs, hidden_refs, d_trans_refs, mixed_refs, d_att_refs, d_cond_refs = pairs
+    cond_ref = refs[14]
+    place = 0
+    tiles = out_refs[0].shape[0]
+    stride = out_refs[0].shape[1] // 2
+    for left, right_refs in (
+        (turned(rows_of(x_refs)), d_up_refs),
+        (turned(rows_of(hidden_refs)), d_trans_refs),
+        (jnp.concatenate([mixed_refs[0][...], mixed_refs[1][...]], axis=1), d_att_refs),
+    ):
+        rows = left.shape[0] // tiles
+        per_blk = right_refs[0].shape[1] // (2 * TILE_COLS)
+        for chunk in range(2 * per_blk):
+            span = slice(chunk * TILE_COLS, (chunk + 1) * TILE_COLS)
+            right = jnp.concatenate([right_refs[0][:, span], right_refs[1][:, span]], axis=0)
+            start = chunk // per_blk * stride + place + chunk % per_blk * rows
+            store_tiles(out_refs, None, nn_dot(left, right), start)
+        place += per_blk * rows
+    cond_tiles(out_refs, None, turned(cond_ref[...]), rows_of(d_cond_refs), place, stride)
+
+
+def rows_of(refs):
+    return jnp.concatenate([refs[0][...], refs[1][...]], axis=0)
+
+
+def early_grads(samp, operands, cond_in):
+    x_trans, d_up, hidden, d_trans, mixed, d_att, d_cond = (pair[0] for pair in operands)
+    sizes = [
+        x_trans.shape[1] * d_up.shape[1],
+        hidden.shape[1] * d_trans.shape[1],
+        mixed.shape[0] * d_att.shape[1],
+        cond_in.shape[1] * d_cond.shape[1],
+    ]
+    rows = 16 * math.ceil(sum(sizes) / (samp * 2 * TILE_COLS * 16))
+    vmem = pl.BlockSpec(memory_space=pltpu.VMEM)
+    return pl.pallas_call(
+        early_grads_kernel,
+        in_specs=[vmem] * (2 * len(operands) + 1),
+        out_specs=vmem,
+        out_shape=jax.ShapeDtypeStruct((samp, 2 * rows, TILE_COLS), jnp.bfloat16),
+        compiler_params=pltpu.CompilerParams(vmem_limit_bytes=VMEM_BYTES),
+        cost_estimate=spends(15),
+        name="early_grads",
+    )(*[value for pair in operands for value in pair], cond_in)
+
+
+def norm_parts(value):
+    center = value - jnp.mean(value, axis=1, keepdims=True)
+    rstd = lax.rsqrt(jnp.mean(center * center, axis=1, keepdims=True) + EPS)
+    return center * rstd, rstd
+
+
+def norm_grad(grad, hat, rstd):
+    inner = jnp.mean(grad * hat, axis=1, keepdims=True)
+    return rstd * (grad - jnp.mean(grad, axis=1, keepdims=True) - hat * inner)
+
+
+def sigmoid(value):
+    return 1.0 / (1.0 + jnp.exp(-value))
+
+
+def first_kernel(
+    place_ref, single_ref, act_ref, cond_weight_ref, cond_bias_ref, gain_ref, weight_ref,
+    query_bias_ref, qkv_ref, gate_t_ref, x_ref, scale_ref, gate_ref, *, score_scale,
+):
+    heads = qkv_ref.shape[0]
+    head_dim = qkv_ref.shape[1] // 3
+    tokens, width = act_ref.shape
+    single_hat, _ = norm_parts(single_ref[place_ref[1]].astype(jnp.float32))
+    cond_in = (single_hat * gain_ref[...]).astype(jnp.bfloat16)
+    bias = cond_bias_ref[...]
+    scale = sigmoid(nn_dot(cond_in, cond_weight_ref[0, :, :width]) + bias[:, :width])
+    scale_ref[...] = scale
+    shift = nn_dot(cond_in, cond_weight_ref[0, :, width : 2 * width])
+    gate_ref[...] = sigmoid(nn_dot(cond_in, cond_weight_ref[0, :, 2 * width :]) + bias[:, width:])
+    act_hat, _ = norm_parts(act_ref[...].astype(jnp.float32))
+    x_attn = (scale * act_hat + shift).astype(jnp.bfloat16)
+    x_ref[...] = x_attn
+    for part in range(4):
+        value = nn_dot(x_attn, weight_ref[:, part * width : (part + 1) * width])
+        if part == 0:
+            value = (value + query_bias_ref[...]) * (score_scale * LOG2E)
+        value = value.T
+        if part == 3:
+            gate_t_ref[...] = sigmoid(value)
+        else:
+            value = value.reshape(heads, head_dim, tokens).astype(jnp.bfloat16)
+            qkv_ref[:, part * head_dim : (part + 1) * head_dim] = value
+
+
+def first_call(heads, place, single_cond, act, cond_weight, cond_bias, gain, weight, query_bias):
+    tokens, width = act.shape
+    head_dim = width // heads
+    vmem = pl.BlockSpec(memory_space=pltpu.VMEM)
+    wide = jax.ShapeDtypeStruct((tokens, width), jnp.float32)
+    return pl.pallas_call(
+        functools.partial(first_kernel, score_scale=1.0 / math.sqrt(head_dim)),
+        grid=(1,),
+        in_specs=[
+            pl.BlockSpec(memory_space=pltpu.SMEM),
+            vmem,
+            vmem,
+            pl.BlockSpec((1,) + cond_weight.shape[1:], lambda _: (0, 0, 0)),
+            vmem,
+            vmem,
+            vmem,
+            vmem,
+        ],
+        out_specs=[vmem] * 5,
+        out_shape=[
+            jax.ShapeDtypeStruct((heads, 3 * head_dim, tokens), jnp.bfloat16),
+            jax.ShapeDtypeStruct((width, tokens), jnp.float32),
+            jax.ShapeDtypeStruct((tokens, width), jnp.bfloat16),
+            wide,
+            wide,
+        ],
+        compiler_params=pltpu.CompilerParams(vmem_limit_bytes=VMEM_BYTES),
+        cost_estimate=spends(12),
+        name="first",
+    )(place, single_cond, act, cond_weight, cond_bias, gain, weight, query_bias)
+
+
+def middle_kernel(
+    attn_ref, gate_t_ref, act_ref, gate_attn_ref, cond_ref, cotangent_ref,
+    out_weight_ref, in_weight_ref, down_weight_ref,
+    block_ref, x_ref, d_up_ref, hid_ref, d_trans_ref, mixed_ref, d_att_ref, d_cond_ref,
+    d_hidden_ref, d_cond_gate_ref, d_gate_ref, d_attn_ref,
+):
+    tokens, width = act_ref.shape
+    units = hid_ref.shape[1]
+    attn = attn_ref[...].reshape(width, tokens).astype(jnp.float32)
+    gate = gate_t_ref[...]
+    mixed = gate * attn
+    mixed_ref[...] = mixed.astype(jnp.bfloat16)
+    att_out = nn_dot(mixed.T.astype(jnp.bfloat16), out_weight_ref[...])
+    gate_attn = gate_attn_ref[...]
+    hidden = act_ref[...].astype(jnp.float32) + gate_attn * att_out
+    hat, rstd = norm_parts(hidden)
+    scale = sigmoid(cond_ref[:, :width])
+    x_trans = (scale * hat + cond_ref[:, width : 2 * width]).astype(jnp.bfloat16)
+    x_ref[...] = x_trans
+    up_gate = nn_dot(x_trans, in_weight_ref[:, :units])
+    up_lin = nn_dot(x_trans, in_weight_ref[:, units:])
+    sig = sigmoid(up_gate)
+    silu = up_gate * sig
+    hid = (silu * up_lin).astype(jnp.bfloat16)
+    hid_ref[...] = hid
+    gate_trans = sigmoid(cond_ref[:, 2 * width :])
+    cotangent = cotangent_ref[...].astype(jnp.float32)
+    gated = gate_trans * cotangent
+    d_trans = gated.astype(jnp.bfloat16)
+    d_trans_ref[...] = d_trans
+    d_hid = nt_dot(d_trans, down_weight_ref[...])
+    slope = sig * (1.0 + up_gate * (1.0 - sig))
+    d_up_ref[:, :units] = (d_hid * up_lin * slope).astype(jnp.bfloat16)
+    d_up_ref[:, units:] = (d_hid * silu).astype(jnp.bfloat16)
+    d_xt = nt_dot(d_up_ref[...], in_weight_ref[...])
+    scaled = d_xt * scale
+    d_hidden = cotangent + norm_grad(scaled, hat, rstd)
+    d_hidden_ref[...] = d_hidden
+    d_att = (gate_attn * d_hidden).astype(jnp.bfloat16)
+    d_att_ref[...] = d_att
+    d_mixed = nt_dot(out_weight_ref[...], d_att)
+    d_attn_ref[...] = (gate * d_mixed).astype(jnp.bfloat16).reshape(d_attn_ref.shape)
+    d_gate_ref[...] = (d_mixed * mixed * (1.0 - gate)).astype(jnp.bfloat16)
+    d_cond_gate_ref[...] = (d_hidden * att_out * gate_attn * (1.0 - gate_attn)).astype(jnp.bfloat16)
+    trans = nn_dot(hid, down_weight_ref[...])
+    block_ref[...] = (hidden + gate_trans * trans).astype(jnp.bfloat16)
+    d_cond_ref[:, :width] = (scaled * hat * (1.0 - scale)).astype(jnp.bfloat16)
+    d_cond_ref[:, width : 2 * width] = d_xt.astype(jnp.bfloat16)
+    d_cond_ref[:, 2 * width :] = (gated * trans * (1.0 - gate_trans)).astype(jnp.bfloat16)
+
+
+def middle_call(half, attn, gate_t, act, gate_attn, cond, cotangent, *weights):
+    tile = attn.shape[2]
+    width = act.shape[1]
+    units = weights[2].shape[0]
+    once = pl.Buffered(1)
+
+    def whole(value):
+        zeros = (0,) * value.ndim
+        return pl.BlockSpec(value.shape, lambda _: zeros, pipeline_mode=once)
+
+    def rows(value):
+        return pl.BlockSpec((tile, value.shape[1]), lambda _: (half, 0), pipeline_mode=once)
+
+    shapes = [
+        jax.ShapeDtypeStruct((tile, width), jnp.bfloat16),
+        jax.ShapeDtypeStruct((tile, width), jnp.bfloat16),
+        jax.ShapeDtypeStruct((tile, 2 * units), jnp.bfloat16),
+        jax.ShapeDtypeStruct((tile, units), jnp.bfloat16),
+        jax.ShapeDtypeStruct((tile, width), jnp.bfloat16),
+        jax.ShapeDtypeStruct((width, tile), jnp.bfloat16),
+        jax.ShapeDtypeStruct((tile, width), jnp.bfloat16),
+        jax.ShapeDtypeStruct((tile, 3 * width), jnp.bfloat16),
+        jax.ShapeDtypeStruct((tile, width), jnp.float32),
+        jax.ShapeDtypeStruct((tile, width), jnp.bfloat16),
+        jax.ShapeDtypeStruct((width, tile), jnp.bfloat16),
+        jax.ShapeDtypeStruct(attn.shape, jnp.bfloat16),
+    ]
+    return pl.pallas_call(
+        middle_kernel,
+        grid=(1,),
+        in_specs=[
+            whole(attn),
+            pl.BlockSpec((width, tile), lambda _: (0, half), pipeline_mode=once),
+            rows(act), rows(gate_attn), rows(cond), rows(cotangent),
+        ]
+        + [whole(weight) for weight in weights],
+        out_specs=[whole(shape) for shape in shapes],
+        out_shape=shapes,
+        compiler_params=pltpu.CompilerParams(vmem_limit_bytes=VMEM_BYTES),
+        cost_estimate=spends(10),
+        name="middle",
+    )(attn, gate_t, act, gate_attn, cond, cotangent, *weights)
+
+
+def final_kernel(
+    place_ref, x_ref, d_query_ref, d_kv_ref, d_gate_one_ref, d_gate_two_ref,
+    weight_ref, act_ref, scale_ref,
+    d_hidden_one_ref, d_hidden_two_ref, d_cond_gate_one_ref, d_cond_gate_two_ref, single_ref, d_hat_ref, cond_weight_ref, gain_ref,
+    act_grad_ref, keep_one_ref, give_one_ref, keep_two_ref, give_two_ref, cond_sums_ref, query_sums_ref, gain_sums_ref,
+    d_cond_ref,
+):
+    core = place_ref[0]
+    struct = place_ref[1]
+    ones = jnp.ones((8, x_ref.shape[0]), jnp.bfloat16)
+    left = turned(x_ref[...])
+    width, tokens = left.shape
+    groups = keep_one_ref.shape[0]
+    rows = width // (2 * groups)
+    head_dim = d_query_ref.shape[1] // 2
+    one = (keep_one_ref, give_one_ref)
+    two = (keep_two_ref, give_two_ref)
+    stride_one = keep_one_ref.shape[1] // 2
+    share = tokens // (2 * groups)
+    stride_two = (keep_two_ref.shape[1] - 2 * share) // 2
+    first_slots = stride_one // rows
+    d_xa = 0.0
+    for part in range(4):
+        if part == 0:
+            right = jnp.concatenate(
+                [d_query_ref[:, :head_dim], d_query_ref[:, head_dim:]], axis=2
+            )
+            right = right.reshape(width, tokens)
+            query_sums_ref[...] = nt_dot(ones, right)
+        elif part == 3:
+            right = jnp.concatenate([d_gate_one_ref[...], d_gate_two_ref[...]], axis=1)
+        else:
+            right = d_kv_ref[:, (part - 1) * head_dim : part * head_dim].reshape(width, tokens)
+        d_xa = d_xa + nn_dot(weight_ref[:, part * width : (part + 1) * width], right)
+        for chunk in range(2):
+            grad = nt_dot(left, right[chunk * TILE_COLS : (chunk + 1) * TILE_COLS])
+            slot = 2 * (part % 2) + chunk
+            if slot < first_slots:
+                store_tiles(one, core, grad, part // 2 * stride_one + slot * rows)
+            else:
+                start = part // 2 * stride_two + (slot - first_slots) * rows
+                store_tiles(two, core, grad, start)
+    d_xa = d_xa.T
+    act_hat, act_rstd = norm_parts(act_ref[...].astype(jnp.float32))
+    scale = scale_ref[...].astype(jnp.float32)
+    grad = d_xa * scale
+    d_hidden = rows_of((d_hidden_one_ref, d_hidden_two_ref))
+    act_grad_ref[...] = d_hidden + norm_grad(grad, act_hat, act_rstd)
+    d_cond_ref[:, :width] = (grad * act_hat * (1.0 - scale)).astype(jnp.bfloat16)
+    d_cond_ref[:, width : 2 * width] = d_xa.astype(jnp.bfloat16)
+    d_cond_ref[:, 2 * width :] = rows_of((d_cond_gate_one_ref, d_cond_gate_two_ref))
+    single_hat, single_rstd = norm_parts(single_ref[...].astype(jnp.float32))
+    gain = gain_ref[...]
+    cond_t = turned((single_hat * gain).astype(jnp.bfloat16))
+    cond_tiles(two, core, cond_t, d_cond_ref, (4 - first_slots) * rows, stride_two)
+    d_cond = d_cond_ref[...]
+    cond_sums_ref[...] = nn_dot(ones, d_cond)
+    d_in = nt_dot(d_cond, cond_weight_ref[...])
+    gain_sums_ref[...] = jnp.sum(d_in * single_hat, axis=0, keepdims=True)
+    single_grad = norm_grad(d_in * gain + d_hat_ref[...], single_hat, single_rstd)
+    single_grad = single_grad.reshape(2 * groups, share, single_grad.shape[1])
+    chosen = [jnp.where(struct == member, single_grad, 0.0) for member in range(2)]
+    chosen = jnp.concatenate(chosen, axis=1).reshape(-1, single_grad.shape[2])
+    store_tiles(two, core, chosen, 2 * stride_two)
+
+
+def final_call(samp, place, x_attn, d_query, d_kv, d_gate, weight, act, scale, d_hidden,
+               d_cond_gate, single, d_hat, cond_weight, gain):
+    groups = samp // 2
+    tokens, width = act.shape
+    chans = single.shape[1]
+    rows = width // samp
+    one_rows = 3 * rows
+    cond_rows = cond_weight.size // (samp * 2 * TILE_COLS)
+    two_rows = rows + 16 * math.ceil(cond_rows / 16)
+    vmem = pl.BlockSpec(memory_space=pltpu.VMEM)
+    share = tokens // samp
+    one = jax.ShapeDtypeStruct((groups, 2 * one_rows, TILE_COLS), jnp.bfloat16)
+    two = jax.ShapeDtypeStruct((groups, 2 * (two_rows + share), TILE_COLS), jnp.bfloat16)
+    return pl.pallas_call(
+        final_kernel,
+        in_specs=[pl.BlockSpec(memory_space=pltpu.SMEM)] + [vmem] * 16,
+        out_specs=[vmem] * 8,
+        out_shape=[
+            jax.ShapeDtypeStruct((tokens, width), jnp.float32),
+            one, one, two, two,
+            jax.ShapeDtypeStruct((8, 3 * width), jnp.float32),
+            jax.ShapeDtypeStruct((8, width), jnp.float32),
+            jax.ShapeDtypeStruct((1, chans), jnp.float32),
+        ],
+        scratch_shapes=[pltpu.VMEM((tokens, 3 * width), jnp.bfloat16)],
+        compiler_params=pltpu.CompilerParams(vmem_limit_bytes=VMEM_BYTES),
+        cost_estimate=spends(20),
+        name="final",
+    )(place, x_attn, d_query, d_kv, *d_gate, weight, act, scale, *d_hidden,
+      *d_cond_gate, single, d_hat, cond_weight, gain)
+
+
+def tie(*values):
+    return lax.optimization_barrier(values)
+
+
+def flip(value, axis, distance):
+    size = lax.axis_size(axis)
+    return lax.ppermute(value, axis, [(i, i ^ distance) for i in range(size)])
+
+
+def halve(value, axis, distance, dim):
+    bit = (lax.axis_index(axis) // distance) % 2
+    keep = lax.dynamic_index_in_dim(value, bit, dim, keepdims=False)
+    give = lax.dynamic_index_in_dim(value, 1 - bit, dim, keepdims=False)
+    return add_low(keep, flip(give, axis, distance))
+
+
+def spread(value, distance, dim):
+    other = flip(value, "samp", distance)
+    first = (lax.axis_index("samp") // distance) % 2 == 0
+    return jnp.stack([jnp.where(first, value, other), jnp.where(first, other, value)], axis=dim)
+
+
+def add_low(left, right):
+    return (left.astype(jnp.float32) + right.astype(jnp.float32)).astype(jnp.bfloat16)
+
+
+def grad_from_tiles(tiles, rows):
+    blocks = tiles.reshape(-1, rows, TILE_COLS)
+    return blocks.transpose(1, 0, 2).reshape(rows, -1)
+
+
+def exchange(value):
+    return lax.all_to_all(value, "samp", 0, 0, tiled=True)
+
+
+def fast_local(
+    activations,
+    single_cond,
+    pair_repr,
+    struct_id,
+    seq_lengths,
+    qkvg_weight,
+    query_bias,
+    out_weight,
+    in_weight,
+    down_weight,
+    cond_weight,
+    cond_bias,
+    single_gain,
+    pair_gain,
+    pair_weight,
+    cotangent,
+):
+    samp = lax.axis_size("samp")
+    blks = lax.axis_size("blk")
+    tokens, width = activations.shape[1:]
+    heads = pair_weight.shape[1]
+    head_dim = width // heads
+    hidden_units = down_weight.shape[0]
+    structs, _, cols, chans = pair_repr.shape
+    blk_arg = lax.axis_index("blk").astype(jnp.int32)[None]
+    index = lax.axis_index("samp").astype(jnp.int32)
+    place = jnp.stack([index % 2, struct_id[0]])
+    act = activations[0]
+
+    qkv, gate_val, x_attn, scale_attn, gate_attn = first_call(
+        heads, place, single_cond, act, cond_weight, cond_bias[:1], single_gain[:1],
+        qkvg_weight, query_bias[None],
+    )
+    own_id = jnp.where(
+        lax.broadcasted_iota(jnp.int32, (8, 128), 1) == index, struct_id[0], 0
+    ).astype(jnp.float32)
+    qkv, pair_in, own_id = tie(qkv, pair_repr, own_id)
+    pair = pair_in.reshape(structs, 2, 2, tokens // 4, cols, chans)
+    bias_part, pair_mean, pair_rstd = pair_forward(pair, pair_gain, pair_weight)
+    own_id, bias_sent = tie(own_id, bias_part)
+    for distance in (1, 2, 4):
+        own_id = own_id + flip(own_id, "samp", distance)
+    qkv, own_id, bias_sent = tie(exchange(qkv), own_id, bias_sent)
+    single = jnp.where(struct_id[0] == 1, single_cond[1], single_cond[0])
+    single_hat = norm_rows(single.astype(jnp.float32))
+    cond_in = (single_hat * single_gain[1]).astype(jnp.bfloat16)
+    bias_row = jnp.concatenate(
+        [cond_bias[1, :width], jnp.zeros((width,), jnp.float32), cond_bias[1, width:]]
+    )
+    cond_trans = nn_dot(cond_in, cond_weight[1]) + bias_row
+    own_id = own_id + flip(own_id, "samp", 8)
+    bias, kv_far, cond_trans, own_id = tie(
+        exchange(bias_sent), flip(qkv[:, head_dim:], "blk", 1), cond_trans, own_id
+    )
+    ids = own_id[0, :samp].astype(jnp.int32)
+    forward_args = (ids, seq_lengths, blk_arg, qkv, kv_far)
+    sent_one, *saved_one = attention_forward(0, *forward_args, bias)
+    sent_one, bias = tie(sent_one, bias)
+    sent_two, *saved_two = attention_forward(1, *forward_args, bias)
+    attn_one, sent_two = tie(exchange(sent_one), sent_two)
+    middle_args = (
+        gate_val, act, gate_attn, cond_trans, cotangent[0], out_weight, in_weight, down_weight
+    )
+    *middle_one, d_attn_one = middle_call(0, attn_one, *middle_args)
+    attn_two, d_attn_one = tie(exchange(sent_two), d_attn_one)
+    *middle_two, d_attn_two = middle_call(1, attn_two, *middle_args)
+    d_attn_one, d_attn_two, *middle_two = tie(exchange(d_attn_one), d_attn_two, *middle_two)
+    both = list(zip(middle_one, middle_two))
+    block_out = jnp.concatenate(both[0], axis=0)
+    d_hidden, d_cond_gate, d_gate_pre = both[8:]
+
+    backward_args = (ids, blk_arg, qkv, kv_far)
+    d_query_one, d_own, d_far, d_bias_one = attention_backward(
+        0, *backward_args, d_attn_one, *saved_one, bias, ()
+    )
+    d_attn_two, d_query_one, d_own, d_far = tie(exchange(d_attn_two), d_query_one, d_own, d_far)
+    d_query_two, d_own, d_far, d_bias_two = attention_backward(
+        1, *backward_args, d_attn_two, *saved_two, bias, (d_own, d_far)
+    )
+    d_query = jnp.concatenate([d_query_one, d_query_two], axis=1)
+    d_bias = jnp.stack([d_bias_one, d_bias_two], axis=1)
+    d_far, d_bias, *operands = tie(d_far, d_bias, *[value for pair in both[1:8] for value in pair])
+    operands = list(zip(operands[::2], operands[1::2]))
+    early = early_grads(samp, operands, cond_in)
+    d_cond_one, d_cond_two = operands[6]
+    d_cond_trans = jnp.concatenate([d_cond_one, d_cond_two], axis=0)
+    d_in = nt_dot(d_cond_trans, cond_weight[1])
+    gain_sums_trans = jnp.sum(d_in * single_hat, axis=0)
+    cond_sums_trans = jnp.sum(d_cond_trans.astype(jnp.float32), axis=0)
+    d_hat = d_in * single_gain[1]
+    d_kv = add_low(d_own, flip(d_far, "blk", 1))
+    d_kv, d_query, d_hat, gain_sums_trans, cond_sums_trans, early, d_bias = tie(
+        d_kv, exchange(d_query), d_hat, gain_sums_trans, cond_sums_trans, early, d_bias
+    )
+    early = lax.psum_scatter(
+        early.reshape(samp * blks, -1, TILE_COLS), ("samp", "blk"), scatter_dimension=0, tiled=True
+    )[0]
+    d_kv, d_bias = tie(exchange(d_kv), d_bias)
+    d_bias = exchange(d_bias)
+
+    (
+        act_grad, keep_one, give_one, keep_two, give_two, cond_sums_attn, query_sums, gain_sums_attn,
+    ) = final_call(
+        samp, place, x_attn, d_query, d_kv, d_gate_pre, qkvg_weight, act, scale_attn,
+        d_hidden, d_cond_gate, single, d_hat, cond_weight[0], single_gain[0][None],
+    )
+    cube = (samp // 8, 2, 2)
+    one = add_low(keep_one, flip(give_one, "samp", 1)).reshape(cube + (2, -1, TILE_COLS))
+    two = add_low(keep_two, flip(give_two, "samp", 1)).reshape(cube + (-1, TILE_COLS))
+    one, two, d_bias = tie(one, two, d_bias)
+    pair_grad, weight_grad_one, gain_grad_one = pair_backward(
+        0, pair, d_bias, bias_part, pair_mean, pair_rstd, pair_gain, pair_weight, ()
+    )
+    one = halve(one, "blk", 1, 3)
+    two = halve(two, "samp", 2, 2)
+    one, two, d_bias, pair_grad = tie(one, two, d_bias, pair_grad)
+    pair_grad, weight_grad_two, gain_grad_two = pair_backward(
+        1, pair, d_bias, bias_part, pair_mean, pair_rstd, pair_gain, pair_weight, (pair_grad,)
+    )
+    shared = 2 * tokens // samp
+    alone = two[:, :, -shared:]
+    two = two[:, :, :-shared].reshape(two.shape[:2] + (2, -1, TILE_COLS))
+    one = halve(one, "samp", 2, 2)
+    two = halve(two, "blk", 1, 2)
+    alone = add_low(alone, flip(alone, "samp", 4))
+    one, two, alone, early, pair_grad, weight_grad_two, gain_grad_two = tie(
+        one, two, alone, early, pair_grad, weight_grad_two, gain_grad_two
+    )
+    small = [
+        query_sums[0],
+        cond_sums_attn[0, :width], cond_sums_attn[0, 2 * width :],
+        cond_sums_trans[:width], cond_sums_trans[2 * width :],
+        gain_sums_attn[0], gain_sums_trans,
+        gain_grad_one + gain_grad_two, (weight_grad_one + weight_grad_two).reshape(-1),
+    ]
+    summed = jnp.concatenate(small)
+    late = halve(jnp.concatenate([one, two], axis=2), "samp", 4, 1)
+    alone = add_low(alone, flip(alone, "samp", 8))
+    summed = summed + flip(summed, "samp", 1)
+    summed = summed + flip(summed, "blk", 1)
+    late, alone, summed = tie(late, alone, summed)
+    late = halve(late, "samp", 8, 0).astype(jnp.float32)
+    alone = spread(alone, 2, 2)
+    summed = summed + flip(summed, "samp", 2)
+    late, alone, summed = tie(late, alone, summed)
+    alone = spread(alone, 1, 3)
+    summed = summed + flip(summed, "samp", 4)
+    summed = summed + flip(summed, "samp", 8)
+    single_grad = alone.reshape(samp, structs, tokens // samp, -1).transpose(1, 0, 2, 3)
+    single_grad = single_grad.reshape(structs, tokens, -1).astype(jnp.float32)
+    early = early.astype(jnp.float32)
+    small_grads = []
+    start = 0
+    for like in (query_bias, cond_bias, single_gain, pair_gain, pair_weight):
+        small_grads.append(summed[start : start + like.size].reshape(like.shape))
+        start += like.size
+    query_bias_grad, cond_bias_grad, single_gain_grad, pair_gain_grad, pair_weight_grad = small_grads
+
+    def take(tiles, start, rows, width_out):
+        count = rows * width_out // TILE_COLS
+        return grad_from_tiles(tiles[start : start + count], rows), start + count
+
+    start = 0
+    in_grad, start = take(early, start, width // samp, in_weight.shape[1] // blks)
+    down_grad, start = take(early, start, hidden_units // samp, width // blks)
+    out_grad, start = take(early, start, width // samp, width // blks)
+    cond_rows_dev = cond_weight.shape[1] // samp
+    cond_cols_dev = cond_weight.shape[2] // blks
+    cond_trans_grad, start = take(early, start, cond_rows_dev, cond_cols_dev)
+    qkvg_grad, start = take(late, 0, width // samp, qkvg_weight.shape[1] // blks)
+    cond_attn_grad, start = take(late, start, cond_rows_dev, cond_cols_dev)
+    return (
+        block_out[None],
+        act_grad[None],
+        single_grad,
+        pair_grad.reshape(pair_repr.shape),
+        qkvg_grad,
+        query_bias_grad,
+        out_grad,
+        in_grad,
+        down_grad,
+        jnp.stack([cond_attn_grad, cond_trans_grad]),
+        cond_bias_grad,
+        single_gain_grad,
+        pair_gain_grad,
+        pair_weight_grad,
+    )
+
+
 def solution(mesh):
+    sizes = dict(mesh.shape)
+    program = fast_local if (sizes["samp"], sizes["blk"]) == (16, 2) else local
     return jax.shard_map(
-        local,
+        program,
         mesh=mesh,
         in_specs=(
             P("samp", "blk", None),

time: 1790 us -> 529 us (0.30)
  waiting for transfers between devices: 1140 us -> 161 us
  matrix products: 236 us -> 7.43 us
  Pallas kernels: 0 us -> 176 us
  local copies, waits for them, and re-layouts: 180 us -> 29.6 us
  other arithmetic: 154 us -> 27.1 us
  starting transfers between devices: 1.24 us -> 100 us
  blocking collectives: 39.7 us -> 0 us
    reduce_scatter x9 -> x1, waiting for transfers between devices: 798 us -> 1.68 us  [fast_local(): lax.psum_scatter(early.reshape(samp * blks, -1, TILE_COLS), ('samp', 'blk...]
    dot_general x35 -> x2, matrix products: 236 us -> 7.43 us  [the longest x1 5.01 us: nn_dot(): lax.dot_general(left, right, (((1,), (0,)), ((), ())), preferred_element_...]
    all_gather x3 -> x0, waiting for transfers between devices: 201 us -> none  [the longest x1 162 us: local(): bias_all = lax.all_gather(bias_local, 'samp', axis=3, tiled=True)]
    pallas_call x0 -> x12, Pallas kernels: none -> 176 us  [the longest x2 28.8 us: pair_backward(): pl.pallas_call(pair_backward_kernel, grid=(structs, half_rows // step), i...]
    unnamed x20 -> x1, waiting for transfers between devices: 144 us -> 0.02 us
    unnamed x163 -> x82, local copies, waits for them, and re-layouts: 142 us -> 5.75 us
    ppermute x0 -> x23, waiting for transfers between devices: none -> 91.4 us  [flip(): return lax.ppermute(value, axis, [(i, i ^ distance) for i in range(size)])]
    all_to_all x0 -> x9, waiting for transfers between devices: none -> 68.2 us  [exchange(): return lax.all_to_all(value, 'samp', 0, 0, tiled=True)]
  transfers between devices with their start and end apart: 16 -> 33, of which waited for: 15 -> 20; matrix products, arithmetic and copies ran while one was open for 8% -> 10% of each run, Pallas kernels for 0% -> 27%
where the time goes in v1:
time: 529 us; the launch traced here: 518 us
  Pallas kernels  176 us (33%)
  waiting for transfers between devices  161 us (30%)
  starting transfers between devices  100 us (19%)
  local copies, waits for them, and re-layouts  29.6 us (6%)
  other arithmetic  27.1 us (5%)
  between operations  15.9 us (3%)
  matrix products  7.43 us (1%)
    ppermute x23, waiting for transfers between devices, flip(): return lax.ppermute(value, axis, [(i, i ^ distance) for i in range(size)])  91.4 us
    all_to_all x9, waiting for transfers between devices, exchange(): return lax.all_to_all(value, 'samp', 0, 0, tiled=True)  68.2 us
    all_to_all x9, starting transfers between devices, exchange(): return lax.all_to_all(value, 'samp', 0, 0, tiled=True)  63.3 us
    ppermute x23, starting transfers between devices, flip(): return lax.ppermute(value, axis, [(i, i ^ distance) for i in range(size)])  37 us
    pallas_call x2, Pallas kernels, pair_backward(): pl.pallas_call(pair_backward_kernel, grid=(structs, half_rows // step), i...  28.8 us
    pallas_call x2, Pallas kernels, attention_backward(): pl.pallas_call(functools.partial(attention_backward_kernel, score_scale=1...  27.9 us
    pallas_call x2, Pallas kernels, middle_call(): pl.pallas_call(middle_kernel, grid=(1,), in_specs=[whole(attn), pl.BlockS...  25.4 us
    pallas_call x2, Pallas kernels, attention_forward(): pl.pallas_call(attention_forward_kernel, grid_spec=grid_spec, out_shape=[...  25.4 us
  transfers between devices with their start and end apart: 33, of which 20 were waited for; matrix products, arithmetic and copies ran while one was open for 10% of the time, Pallas kernels for 27%

profile of v1, /device:TPU:0, one launch (start us, length us, event | category | flops | bytes accessed | tf_op | source)
XLA Modules:
  0.0 518.3 jit_solution(12916611072080607885)
XLA Ops:
  9.1 1.3 slice_reduce_fusion.5
  12.3 9.9 %first.1 = (bf16[16,144,512]{2,1,0:T(8,128)(2,1)}, f32[768,512]{1,0:T(8,128)}, bf16[512,768]{1,0:T(8,128)(2,1)}, f32[512,768]{1,0:T(8,128)}, f32[512,768]{1,0:T(8,128)}) custom-call(s32[2]{0:T(128)} %pad_add_fusion.place_ref, bf16[2,512,384]{2,1,0:T(8,128)(2,1)} %single_ref.1, bf16[512,768]{1,0:T(8,128)(2,1)} %bitcast.154, ...), custom_call_target="tpu_custom_call" | custom-call | flops 12000000000 | bytes 36000000 | tf_op jit(solution)/shard_map/first/pallas_call | solution.py:936
  22.2 7.5 %all-to-all-start = ((bf16[16,144,512]{2,1,0:T(8,128)(2,1)}), bf16[16,144,512]{2,1,0:T(8,128)(2,1)S(1)}, u32[]{:S(2)}, u32[]{:S(2)}) async-start(bf16[16,144,512]{2,1,0:T(8,128)(2,1)} %get-tuple-element.169), calls=%async_computation | async-start | bytes 4718592 | tf_op jit(solution)/shard_map/all_to_all | solution.py:1188
  31.2 20.6 %pair_forward.1 = (bf16[16,2,2,128,128]{4,3,2,1,0:T(8,128)(2,1)}, f32[2,2,128,128]{3,2,1,0:T(8,128)}, f32[2,2,128,128]{3,2,1,0:T(8,128)}) custom-call(bf16[2,2,2,128,64,128]{5,4,3,2,1,0:T(8,128)(2,1)} %bitcast.125, bf16[48,256]{1,0:T(8,128)(2,1)} %pad_maximum_fusion.5.coef_ref, f32[16,1]{1,0:T(8,128)} %copy.51.coef_sum_ref), custom_call_target="tpu_custom_call" | custom-call | flops 20000000000 | bytes 60000000 | tf_op jit(solution)/shard_map/pair_forward/pallas_call | solution.py:480
  53.2 1.9 collective-permute-start.1
  55.1 1.7 collective-permute-done.1
  56.8 1.9 collective-permute-start.2
  58.7 10.3 %collective-permute-done.2 = f32[8,128]{1,0:T(8,128)S(1)} collective-permute-done((f32[8,128]{1,0:T(8,128)S(1)}, f32[8,128]{1,0:T(8,128)S(1)}, u32[]{:S(2)}, u32[]{:S(2)}) %collective-permute-start.2) | collective-permute-done | bytes 4128 | tf_op jit(solution)/shard_map/ppermute | solution.py:1162
  69.0 6.4 %all-to-all-done.query_ref.key_own_ref.value_own_ref = bf16[16,144,512]{2,1,0:T(8,128)(2,1)S(1)} async-done(((bf16[16,144,512]{2,1,0:T(8,128)(2,1)}), bf16[16,144,512]{2,1,0:T(8,128)(2,1)S(1)}, u32[]{:S(2)}, u32[]{:S(2)}) %all-to-all-start) | async-done | bytes 2359328 | tf_op jit(solution)/shard_map/all_to_all | solution.py:1188
  75.4 12.3 %all-to-all-start.1 = ((bf16[16,2,2,128,128]{4,3,2,1,0:T(8,128)(2,1)}), bf16[16,2,2,128,128]{4,3,2,1,0:T(8,128)(2,1)}, u32[]{:S(2)}, u32[]{:S(2)}) async-start(bf16[16,2,2,128,128]{4,3,2,1,0:T(8,128)(2,1)} %get-tuple-element.175.bias_ref), calls=%async_computation.1 | async-start | bytes 4194304 | tf_op jit(solution)/shard_map/all_to_all | solution.py:1188
  89.1 1.5 collective-permute-start.3
  91.1 2.8 collective-permute-start.4
  94.0 5.0 convolution_add_fusion.cond_ref
  99.0 38.0 %collective-permute-done.4 = f32[8,128]{1,0:T(8,128)S(1)} collective-permute-done((f32[8,128]{1,0:T(8,128)S(1)}, f32[8,128]{1,0:T(8,128)S(1)}, u32[]{:S(2)}, u32[]{:S(2)}) %collective-permute-start.4) | collective-permute-done | bytes 4128 | tf_op jit(solution)/shard_map/ppermute | solution.py:1162
  138.1 12.7 %attention_forward.2 = (bf16[16,48,256]{2,1,0:T(8,128)(2,1)}, f32[16,48,256]{2,1,0:T(8,128)}, f32[16,1,256]{2,1,0:T(1,128)}, bf16[16,1024,256]{2,1,0:T(8,128)(2,1)}) custom-call(s32[16]{0:T(128)} %convert_bitcast_fusion.1.ids_ref, s32[2]{0:T(128)} %limits_ref.3, s32[1]{0:T(128)} %bitcast.10.blk_ref, bf16[16,144,512]{2,1,0:T(8,128)(2,1)} %copy-done.2, ...), custom_call_target="tpu_custom_call" | custom-call | flops 14000000000 | bytes 42000000 | tf_op jit(solution)/shard_map/attention_forward/pallas_call | solution.py:682
  150.8 3.9 all-to-all-start.2
  154.7 12.7 %attention_forward.3 = (bf16[16,48,256]{2,1,0:T(8,128)(2,1)}, f32[16,48,256]{2,1,0:T(8,128)}, f32[16,1,256]{2,1,0:T(1,128)}, bf16[16,1024,256]{2,1,0:T(8,128)(2,1)}) custom-call(s32[16]{0:T(128)} %convert_bitcast_fusion.1.ids_ref, s32[2]{0:T(128)} %limits_ref.3, s32[1]{0:T(128)} %bitcast.10.blk_ref, bf16[16,144,512]{2,1,0:T(8,128)(2,1)} %copy-done.2, ...), custom_call_target="tpu_custom_call" | custom-call | flops 14000000000 | bytes 42000000 | tf_op jit(solution)/shard_map/attention_forward/pallas_call | solution.py:682
  167.5 6.1 %all-to-all-start.3 = ((bf16[16,48,256]{2,1,0:T(8,128)(2,1)}), bf16[16,48,256]{2,1,0:T(8,128)(2,1)S(1)}, u32[]{:S(2)}, u32[]{:S(2)}) async-start(bf16[16,48,256]{2,1,0:T(8,128)(2,1)} %get-tuple-element.190), calls=%async_computation.3 | async-start | bytes 786432 | tf_op jit(solution)/shard_map/all_to_all | solution.py:1188
  173.6 12.7 %middle.2 = (bf16[256,768]{1,0:T(8,128)(2,1)}, bf16[256,768]{1,0:T(8,128)(2,1)}, bf16[256,3072]{1,0:T(8,128)(2,1)}, bf16[256,1536]{1,0:T(8,128)(2,1)}, bf16[256,...) custom-call(bf16[16,48,256]{2,1,0:T(8,128)(2,1)} %copy-done.16, ...), custom_call_target="tpu_custom_call" | custom-call | flops 10000000000 | bytes 30000000 | tf_op jit(solution)/shard_map/middle/pallas_call | solution.py:1041
  186.3 6.4 %all-to-all-start.4 = ((bf16[16,48,256]{2,1,0:T(8,128)(2,1)}), bf16[16,48,256]{2,1,0:T(8,128)(2,1)S(1)}, u32[]{:S(2)}, u32[]{:S(2)}) async-start(bf16[16,48,256]{2,1,0:T(8,128)(2,1)} %get-tuple-element.192), calls=%async_computation.4 | async-start | bytes 786432 | tf_op jit(solution)/shard_map/all_to_all | solution.py:1188
  192.8 12.7 %middle.3 = (bf16[256,768]{1,0:T(8,128)(2,1)}, bf16[256,768]{1,0:T(8,128)(2,1)}, bf16[256,3072]{1,0:T(8,128)(2,1)}, bf16[256,1536]{1,0:T(8,128)(2,1)}, bf16[256,...) custom-call(bf16[16,48,256]{2,1,0:T(8,128)(2,1)} %copy-done.14, ...), custom_call_target="tpu_custom_call" | custom-call | flops 10000000000 | bytes 30000000 | tf_op jit(solution)/shard_map/middle/pallas_call | solution.py:1041
  205.5 6.1 %all-to-all-start.5 = ((bf16[16,48,256]{2,1,0:T(8,128)(2,1)}), bf16[16,48,256]{2,1,0:T(8,128)(2,1)S(1)}, u32[]{:S(2)}, u32[]{:S(2)}) async-start(bf16[16,48,256]{2,1,0:T(8,128)(2,1)} %get-tuple-element.208), calls=%async_computation.5 | async-start | bytes 786432 | tf_op jit(solution)/shard_map/all_to_all | solution.py:1188
  211.6 13.8 %attention_backward.2 = (bf16[16,48,256]{2,1,0:T(8,128)(2,1)}, bf16[16,96,512]{2,1,0:T(8,128)(2,1)}, bf16[16,96,512]{2,1,0:T(8,128)(2,1)}, bf16[16,2,128,128]{3,2,1,0:T(8,128)(2,1)}) custom-call(s32[16]{0:T(128)} %convert_bitcast_fusion.1.ids_ref, s32[1]{0:T(128)} %bitcast.10.blk_ref, bf16[16,144,512]{2,1,0:T(8,128)(2,1)} %copy-done.2, ...), custom_call_target="tpu_custom_call" | custom-call | flops 12999999488 | bytes 39000000 | tf_op jit(solution)/shard_map/attention_backward/pallas_call | solution.py:788
  226.1 14.2 %attention_backward.3 = (bf16[16,48,256]{2,1,0:T(8,128)(2,1)}, bf16[16,96,512]{2,1,0:T(8,128)(2,1)}, bf16[16,96,512]{2,1,0:T(8,128)(2,1)}, bf16[16,2,128,128]{3,2,1,0:T(8,128)(2,1)}) custom-call(s32[16]{0:T(128)} %convert_bitcast_fusion.1.ids_ref, s32[1]{0:T(128)} %bitcast.10.blk_ref, bf16[16,144,512]{2,1,0:T(8,128)(2,1)} %copy-done.2, ...), custom_call_target="tpu_custom_call" | custom-call | flops 12999999488 | bytes 39000000 | tf_op jit(solution)/shard_map/attention_backward/pallas_call | solution.py:788
  240.3 2.8 pad_maximum_fusion
  243.1 1.5 collective-permute-start.5
  245.6 6.0 %all-to-all-start.6 = ((bf16[16,96,256]{2,1,0:T(8,128)(2,1)}), bf16[16,96,256]{2,1,0:T(8,128)(2,1)S(1)}, u32[]{:S(2)}, u32[]{:S(2)}) async-start(bf16[16,96,256]{2,1,0:T(8,128)(2,1)} %pad_maximum_fusion.1), calls=%async_computation.6 | async-start | bytes 1572864 | tf_op jit(solution)/shard_map/all_to_all | solution.py:1188
  251.9 1.5 constant_dynamic-update-slice_fusion.1
  253.4 1.3 constant_dynamic-update-slice_fusion
  254.7 2.4 fusion.13
  257.6 15.1 %early_grads.1 = bf16[16,832,384]{2,1,0:T(8,128)(2,1)} custom-call(bf16[256,768]{1,0:T(8,128)(2,1)} %get-tuple-element.245.refs_0_, bf16[256,768]{1,0:T(8,128)(2,1)} %get-tuple-element.246.refs_1_, bf16[256,3072]{1,0:T(8,128)(2,1)} %get-tuple-element.247.refs_2_, bf16[256,3072]{1,0:T(8,128)(2,1)} %get-tuple-element.248.refs_3_, ...), custom_call_target="tpu_custom_call" | custom-call | flops 15000000512 | bytes 45000000 | tf_op jit(solution)/shard_map/early_grads/pallas_call | solution.py:876
  272.7 7.4 %collective-permute-done.5 = bf16[16,96,512]{2,1,0:T(8,128)(2,1)S(1)} collective-permute-done((bf16[16,96,512]{2,1,0:T(8,128)(2,1)}, bf16[16,96,512]{2,1,0:T(8,128)(2,1)S(1)}, u32[]{:S(2)}, u32[]{:S(2)}) %collective-permute-start.5) | collective-permute-done | bytes 1572896 | tf_op jit(solution)/shard_map/ppermute | solution.py:1162
  280.0 1.6 add_convert_fusion.2
  282.6 5.8 %all-to-all-start.7 = ((bf16[16,96,512]{2,1,0:T(8,128)(2,1)}), bf16[16,96,512]{2,1,0:T(8,128)(2,1)S(1)}, u32[]{:S(2)}, u32[]{:S(2)}) async-start(bf16[16,96,512]{2,1,0:T(8,128)(2,1)} %add_convert_fusion.2), calls=%async_computation.7 | async-start | bytes 3145728 | tf_op jit(solution)/shard_map/all_to_all | solution.py:1188
  288.3 2.8 slice_bitcast_fusion.cond_weight_ref
  291.1 29.2 %all-to-all-done.7.d_kv_ref = bf16[16,96,512]{2,1,0:T(8,128)(2,1)S(1)} async-done(((bf16[16,96,512]{2,1,0:T(8,128)(2,1)}), bf16[16,96,512]{2,1,0:T(8,128)(2,1)S(1)}, u32[]{:S(2)}, u32[]{:S(2)}) %all-to-all-start.7) | async-done | bytes 1572896 | tf_op jit(solution)/shard_map/all_to_all | solution.py:1188
  321.5 9.1 %all-to-all-start.8 = ((bf16[16,2,2,128,128]{4,3,2,1,0:T(8,128)(2,1)}), bf16[16,2,2,128,128]{4,3,2,1,0:T(8,128)(2,1)S(1)}, u32[]{:S(2)}, u32[]{:S(2)}) async-start(bf16[16,2,2,128,128]{4,3,2,1,0:T(8,128)(2,1)} %pad_maximum_fusion), calls=%async_computation.8 | async-start | bytes 4194304 | tf_op jit(solution)/shard_map/all_to_all | solution.py:1188
  330.6 23.3 %final.1 = (f32[512,768]{1,0:T(8,128)}, bf16[8,288,384]{2,1,0:T(8,128)(2,1)}, bf16[8,288,384]{2,1,0:T(8,128)(2,1)}, bf16[8,320,384]{2,1,0:T(8,128)(2,1)}, bf16[8...) custom-call(s32[2]{0:T(128)} %pad_add_fusion.place_ref, ...), custom_call_target="tpu_custom_call" | custom-call | flops 20000000000 | bytes 60000000 | tf_op jit(solution)/shard_map/final/pallas_call | solution.py:1137
  358.1 3.8 add_convert_fusion.1
  361.9 3.4 add_convert_fusion
  365.3 32.6 %all-to-all-done.8.d_bias_ref = bf16[16,2,2,128,128]{4,3,2,1,0:T(8,128)(2,1)S(1)} async-done(((bf16[16,2,2,128,128]{4,3,2,1,0:T(8,128)(2,1)}), bf16[16,2,2,128,128]{4,3,2,1,0:T(8,128)(2,1)S(1)}, u32[]{:S(2)}, u32[]{:S(2)}) %all-to-all-start.8) | async-done | bytes 2097184 | tf_op jit(solution)/shard_map/all_to_all | solution.py:1188
  397.9 2.9 copy_bitcast_fusion
  400.8 1.5 collective-permute-start.8
  403.6 4.5 collective-permute-start.9
  408.1 14.4 %pair_backward.2 = (f32[2,2,2,128,64,128]{5,4,3,2,1,0:T(8,128)}, f32[32,128]{1,0:T(8,128)}, f32[16,128]{1,0:T(8,128)}) custom-call(bf16[2,2,2,128,64,128]{5,4,3,2,1,0:T(8,128)(2,1)} %bitcast.126, bf16[16,2,2,128,128]{4,3,2,1,0:T(8,128)(2,1)} %copy-done, bf16[16,2,2,128,128]{4,3,2,1,0:T(8,128)(2,1)} %get-tuple-element.175.bias_ref, ...), custom_call_target="tpu_custom_call" | custom-call | flops 12999999488 | bytes 39000000 | tf_op jit(solution)/shard_map/pair_backward/pallas_call | solution.py:558
  423.7 1.7 fusion.1
  425.4 13.5 %collective-permute-done.9 = bf16[2,2,320,384]{3,2,1,0:T(8,128)(2,1)} collective-permute-done((bf16[2,2,320,384]{3,2,1,0:T(8,128)(2,1)S(1)}, bf16[2,2,320,384]{3,2,1,0:T(8,128)(2,1)}, u32[]{:S(2)}, u32[]{:S(2)}) %collective-permute-start.9) | collective-permute-done | bytes 983072 | tf_op jit(solution)/shard_map/ppermute | solution.py:1162
  438.9 1.4 fusion
  441.3 2.6 collective-permute-start.10
  444.1 6.8 %collective-permute-start.12 = (bf16[2,2,64,384]{3,2,1,0:T(8,128)(2,1)S(1)}, bf16[2,2,64,384]{3,2,1,0:T(8,128)(2,1)}, u32[]{:S(2)}, u32[]{:S(2)}) collective-permute-start(bf16[2,2,64,384]{3,2,1,0:T(8,128)(2,1)S(1)} %slice.138), channel_id=1, source_target_pairs={{0,8},{2,10},{4,12},{6,14},{8,0},{10,2},{12,4},{14,6},{16,24},{18,... | collective-permute-start | bytes 589832 | tf_op jit(solution)/shard_map/ppermute | solution.py:1162
  450.9 14.4 %pair_backward.3 = (f32[2,2,2,128,64,128]{5,4,3,2,1,0:T(8,128)}, f32[32,128]{1,0:T(8,128)}, f32[16,128]{1,0:T(8,128)}) custom-call(bf16[2,2,2,128,64,128]{5,4,3,2,1,0:T(8,128)(2,1)} %bitcast.127, bf16[16,2,2,128,128]{4,3,2,1,0:T(8,128)(2,1)} %copy-done, bf16[16,2,2,128,128]{4,3,2,1,0:T(8,128)(2,1)} %get-tuple-element.175.bias_ref, ...), custom_call_target="tpu_custom_call", output_to_operand_aliasing={{0}: (7, {})} | custom-call | flops 12999999488 | bytes 39000000 | tf_op jit(solution)/shard_map/pair_backward/pallas_call | solution.py:558
  469.3 1.7 reduce-scatter.2.cloned.1.call-done
  471.1 1.4 collective-permute-start.13
  472.6 1.7 collective-permute-start.14
  475.8 1.4 collective-permute-start.16
  477.2 2.5 collective-permute-done.16
  479.7 4.1 collective-permute-done.14
  483.8 1.3 collective-permute-done.13
  485.2 1.5 collective-permute-start.18
  487.3 2.1 collective-permute-start.17
  489.5 1.8 collective-permute-done.19
  491.4 6.1 %collective-permute-done.17 = bf16[272,384]{1,0:T(8,128)(2,1)S(1)} collective-permute-done((bf16[272,384]{1,0:T(8,128)(2,1)S(1)}, bf16[272,384]{1,0:T(8,128)(2,1)S(1)}, u32[]{:S(2)}, u32[]{:S(2)}) %collective-permute-start.17) | collective-permute-done | bytes 208928 | tf_op jit(solution)/shard_map/ppermute | solution.py:1162
  501.5 1.9 collective-permute-start.22
  504.9 1.4 collective-permute-done.22
  (197 shorter events, 37.5 us)
Async XLA Ops:
  22.2 7.6 %copy-start.25 = (bf16[128,16]{0,1:T(8,128)(2,1)S(1)}, bf16[128,16]{0,1:T(8,128)(2,1)}, u32[]{:S(2)}) copy-start(bf16[128,16]{0,1:T(8,128)(2,1)} %param.32) | copy-start | bytes 12292
  22.2 7.6 %copy-start.30 = (f32[128]{0:T(128)S(1)}, f32[128]{0:T(128)}, u32[]{:S(2)}) copy-start(f32[128]{0:T(128)} %param.31) | copy-start | bytes 1540
  22.2 8.4 %copy-start.28 = (bf16[48,128]{1,0:T(8,128)(2,1)S(1)}, bf16[48,128]{1,0:T(8,128)(2,1)}, u32[]{:S(2)}) copy-start(bf16[48,128]{1,0:T(8,128)(2,1)} %constant.182.clone.1) | copy-start | bytes 36868
  22.2 8.4 %copy-start.34 = (bf16[8,128]{1,0:T(8,128)(2,1)S(1)}, bf16[8,128]{1,0:T(8,128)(2,1)}, u32[]{:S(2)}) copy-start(bf16[8,128]{1,0:T(8,128)(2,1)} %constant.180.clone.1) | copy-start | bytes 6148
  22.2 53.2 %all-to-all-start = ((bf16[16,144,512]{2,1,0:T(8,128)(2,1)}), bf16[16,144,512]{2,1,0:T(8,128)(2,1)S(1)}, u32[]{:S(2)}, u32[]{:S(2)}) async-start(bf16[16,144,512]{2,1,0:T(8,128)(2,1)} %get-tuple-element.169), calls=%async_computation | async-start | bytes 4718592 | tf_op jit(solution)/shard_map/all_to_all | solution.py:1188
  29.9 22.0 %copy-start.22 = (bf16[16,128]{1,0:T(8,128)(2,1)}, bf16[16,128]{1,0:T(8,128)(2,1)S(1)}, u32[]{:S(2)}) copy-start(bf16[16,128]{1,0:T(8,128)(2,1)S(1)} %get-tuple-element.359) | copy-start | bytes 12292
  29.9 22.0 %copy-start.32 = (f32[16]{0:T(128)}, f32[16]{0:T(128)S(1)}, u32[]{:S(2)}) copy-start(f32[16]{0:T(128)S(1)} %get-tuple-element.358) | copy-start | bytes 196
  51.9 1.3 collective-permute-start
  53.2 3.6 collective-permute-start.1
  56.8 12.2 %collective-permute-start.2 = (f32[8,128]{1,0:T(8,128)S(1)}, f32[8,128]{1,0:T(8,128)S(1)}, u32[]{:S(2)}, u32[]{:S(2)}) collective-permute-start(f32[8,128]{1,0:T(8,128)S(1)} %add.162), channel_id=1, source_target_pairs={{0,8},{2,10},{4,12},{6,14},{8,0},{10,2},{12,4},{14,6},{16,24},{18,... | collective-permute-start | bytes 12296 | tf_op jit(solution)/shard_map/ppermute | solution.py:1162
  75.4 12.3 %copy-start.2 = (bf16[16,144,512]{2,1,0:T(8,128)(2,1)}, bf16[16,144,512]{2,1,0:T(8,128)(2,1)S(1)}, u32[]{:S(2)}) copy-start(bf16[16,144,512]{2,1,0:T(8,128)(2,1)S(1)} %all-to-all-done.query_ref.key_own_ref.value_own_ref) | copy-start | bytes 7077892
  75.4 61.5 %all-to-all-start.1 = ((bf16[16,2,2,128,128]{4,3,2,1,0:T(8,128)(2,1)}), bf16[16,2,2,128,128]{4,3,2,1,0:T(8,128)(2,1)}, u32[]{:S(2)}, u32[]{:S(2)}) async-start(bf16[16,2,2,128,128]{4,3,2,1,0:T(8,128)(2,1)} %get-tuple-element.175.bias_ref), calls=%async_computation.1 | async-start | bytes 4194304 | tf_op jit(solution)/shard_map/all_to_all | solution.py:1188
  87.8 2.8 copy-start.13
  89.1 47.9 %collective-permute-start.3 = (bf16[16,96,512]{2,1,0:T(8,128)(2,1)}, bf16[16,96,512]{2,1,0:T(8,128)(2,1)S(1)}, u32[]{:S(2)}, u32[]{:S(2)}) collective-permute-start(bf16[16,96,512]{2,1,0:T(8,128)(2,1)} %slice.128), channel_id=1, source_target_pairs={{0,1},{1,0},{2,3},{3,2},{4,5},{5,4},{6,7},{7,6},{8,9},{9,8},{10,11... | collective-permute-start | bytes 4718600 | tf_op jit(solution)/shard_map/ppermute | solution.py:1162
  90.8 163.9 %copy-start.7 = (bf16[512,384]{1,0:T(8,128)(2,1)}, bf16[512,384]{1,0:T(8,128)(2,1)S(1)}, u32[]{:S(2)}) copy-start(bf16[512,384]{1,0:T(8,128)(2,1)S(1)} %get-tuple-element.345.single_ref) | copy-start | bytes 1179652
  91.1 45.8 %collective-permute-start.4 = (f32[8,128]{1,0:T(8,128)S(1)}, f32[8,128]{1,0:T(8,128)S(1)}, u32[]{:S(2)}, u32[]{:S(2)}) collective-permute-start(f32[8,128]{1,0:T(8,128)S(1)} %add.163), channel_id=1, source_target_pairs={{0,16},{2,18},{4,20},{6,22},{8,24},{10,26},{12,28},{14,30},{16,0},... | collective-permute-start | bytes 12296 | tf_op jit(solution)/shard_map/ppermute | solution.py:1162
  150.8 16.6 %all-to-all-start.2 = ((bf16[16,48,256]{2,1,0:T(8,128)(2,1)}), bf16[16,48,256]{2,1,0:T(8,128)(2,1)S(1)}, u32[]{:S(2)}, u32[]{:S(2)}) async-start(bf16[16,48,256]{2,1,0:T(8,128)(2,1)} %get-tuple-element.182), calls=%async_computation.2 | async-start | bytes 786432 | tf_op jit(solution)/shard_map/all_to_all | solution.py:1188
  167.5 6.1 %copy-start.16 = (bf16[16,48,256]{2,1,0:T(8,128)(2,1)}, bf16[16,48,256]{2,1,0:T(8,128)(2,1)S(1)}, u32[]{:S(2)}) copy-start(bf16[16,48,256]{2,1,0:T(8,128)(2,1)S(1)} %all-to-all-done.2.attn_ref) | copy-start | bytes 1179652
  167.5 18.9 %all-to-all-start.3 = ((bf16[16,48,256]{2,1,0:T(8,128)(2,1)}), bf16[16,48,256]{2,1,0:T(8,128)(2,1)S(1)}, u32[]{:S(2)}, u32[]{:S(2)}) async-start(bf16[16,48,256]{2,1,0:T(8,128)(2,1)} %get-tuple-element.190), calls=%async_computation.3 | async-start | bytes 786432 | tf_op jit(solution)/shard_map/all_to_all | solution.py:1188
  186.3 6.4 %copy-start.14 = (bf16[16,48,256]{2,1,0:T(8,128)(2,1)}, bf16[16,48,256]{2,1,0:T(8,128)(2,1)S(1)}, u32[]{:S(2)}) copy-start(bf16[16,48,256]{2,1,0:T(8,128)(2,1)S(1)} %all-to-all-done.3.attn_ref) | copy-start | bytes 1179652
  186.3 19.1 %all-to-all-start.4 = ((bf16[16,48,256]{2,1,0:T(8,128)(2,1)}), bf16[16,48,256]{2,1,0:T(8,128)(2,1)S(1)}, u32[]{:S(2)}, u32[]{:S(2)}) async-start(bf16[16,48,256]{2,1,0:T(8,128)(2,1)} %get-tuple-element.192), calls=%async_computation.4 | async-start | bytes 786432 | tf_op jit(solution)/shard_map/all_to_all | solution.py:1188
  205.4 6.1 %copy-start.15 = (bf16[16,48,256]{2,1,0:T(8,128)(2,1)}, bf16[16,48,256]{2,1,0:T(8,128)(2,1)S(1)}, u32[]{:S(2)}) copy-start(bf16[16,48,256]{2,1,0:T(8,128)(2,1)S(1)} %all-to-all-done.4.d_attn_ref) | copy-start | bytes 1179652
  205.5 19.9 %all-to-all-start.5 = ((bf16[16,48,256]{2,1,0:T(8,128)(2,1)}), bf16[16,48,256]{2,1,0:T(8,128)(2,1)S(1)}, u32[]{:S(2)}, u32[]{:S(2)}) async-start(bf16[16,48,256]{2,1,0:T(8,128)(2,1)} %get-tuple-element.208), calls=%async_computation.5 | async-start | bytes 786432 | tf_op jit(solution)/shard_map/all_to_all | solution.py:1188
  226.1 14.2 %copy-start.10 = (bf16[16,2,128,128]{3,2,1,0:T(8,128)(2,1)S(1)}, bf16[16,2,128,128]{3,2,1,0:T(8,128)(2,1)}, u32[]{:S(2)}) copy-start(bf16[16,2,128,128]{3,2,1,0:T(8,128)(2,1)} %get-tuple-element.224) | copy-start | bytes 3145732
  240.3 4.4 copy-start.20
  240.3 4.4 copy-start.21
  243.1 36.9 %collective-permute-start.5 = (bf16[16,96,512]{2,1,0:T(8,128)(2,1)}, bf16[16,96,512]{2,1,0:T(8,128)(2,1)S(1)}, u32[]{:S(2)}, u32[]{:S(2)}) collective-permute-start(bf16[16,96,512]{2,1,0:T(8,128)(2,1)} %get-tuple-element.240), channel_id=1, source_target_pairs={{0,1},{1,0},{2,3},{3,2},{4,5},{5,4},{6,7},{7,6},{8,9},{9,8},{10,11... | collective-permute-start | bytes 4718600 | tf_op jit(solution)/shard_map/ppermute | solution.py:1162
  245.6 36.0 %all-to-all-start.6 = ((bf16[16,96,256]{2,1,0:T(8,128)(2,1)}), bf16[16,96,256]{2,1,0:T(8,128)(2,1)S(1)}, u32[]{:S(2)}, u32[]{:S(2)}) async-start(bf16[16,96,256]{2,1,0:T(8,128)(2,1)} %pad_maximum_fusion.1), calls=%async_computation.6 | async-start | bytes 1572864 | tf_op jit(solution)/shard_map/all_to_all | solution.py:1188
  251.6 219.3 %reduce-scatter.2.cloned.1.call-start = ((), (), s32[]{:S(2)}) async-start(), calls=%async_computation.10 | async-start | bytes 10543104 | tf_op jit(solution)/shard_map/reduce_scatter | solution.py:1286
  251.8 2.9 copy-start.11
  257.6 22.5 %copy-start.8 = (bf16[16,96,512]{2,1,0:T(8,128)(2,1)S(1)}, bf16[16,96,512]{2,1,0:T(8,128)(2,1)}, u32[]{:S(2)}) copy-start(bf16[16,96,512]{2,1,0:T(8,128)(2,1)} %get-tuple-element.222) | copy-start | bytes 4718596
  282.6 37.8 %all-to-all-start.7 = ((bf16[16,96,512]{2,1,0:T(8,128)(2,1)}), bf16[16,96,512]{2,1,0:T(8,128)(2,1)S(1)}, u32[]{:S(2)}, u32[]{:S(2)}) async-start(bf16[16,96,512]{2,1,0:T(8,128)(2,1)} %add_convert_fusion.2), calls=%async_computation.7 | async-start | bytes 3145728 | tf_op jit(solution)/shard_map/all_to_all | solution.py:1188
  321.5 76.5 %all-to-all-start.8 = ((bf16[16,2,2,128,128]{4,3,2,1,0:T(8,128)(2,1)}), bf16[16,2,2,128,128]{4,3,2,1,0:T(8,128)(2,1)S(1)}, u32[]{:S(2)}, u32[]{:S(2)}) async-start(bf16[16,2,2,128,128]{4,3,2,1,0:T(8,128)(2,1)} %pad_maximum_fusion), calls=%async_computation.8 | async-start | bytes 4194304 | tf_op jit(solution)/shard_map/all_to_all | solution.py:1188
  330.6 23.9 %copy-start.33 = (f32[16]{0:T(128)S(1)}, f32[16]{0:T(128)}, u32[]{:S(2)}) copy-start(f32[16]{0:T(128)} %copy-done.32) | copy-start | bytes 196
  330.6 24.6 %copy-start.23 = (bf16[16,128]{1,0:T(8,128)(2,1)S(1)}, bf16[16,128]{1,0:T(8,128)(2,1)}, u32[]{:S(2)}) copy-start(bf16[16,128]{1,0:T(8,128)(2,1)} %copy-done.22) | copy-start | bytes 12292
  330.6 24.7 %copy-start.29 = (bf16[36,128]{1,0:T(8,128)(2,1)S(1)}, bf16[36,128]{1,0:T(8,128)(2,1)}, u32[]{:S(2)}) copy-start(bf16[36,128]{1,0:T(8,128)(2,1)} %constant.189.clone.1) | copy-start | bytes 27652
  353.9 4.1 collective-permute-start.6
  354.4 7.5 %collective-permute-start.7 = (bf16[8,320,384]{2,1,0:T(8,128)(2,1)}, bf16[8,320,384]{2,1,0:T(8,128)(2,1)}, u32[]{:S(2)}, u32[]{:S(2)}) collective-permute-start(bf16[8,320,384]{2,1,0:T(8,128)(2,1)} %get-tuple-element.274), channel_id=1, source_target_pairs={{0,2},{2,0},{4,6},{6,4},{8,10},{10,8},{12,14},{14,12},{16,18},{18,... | collective-permute-start | bytes 5898248 | tf_op jit(solution)/shard_map/ppermute | solution.py:1162
  358.1 3.9 copy-start.5
  397.9 10.2 %copy-start = (bf16[16,2,2,128,128]{4,3,2,1,0:T(8,128)(2,1)}, bf16[16,2,2,128,128]{4,3,2,1,0:T(8,128)(2,1)S(1)}, u32[]{:S(2)}) copy-start(bf16[16,2,2,128,128]{4,3,2,1,0:T(8,128)(2,1)S(1)} %all-to-all-done.8.d_bias_ref) | copy-start | bytes 6291460
  400.8 22.9 %collective-permute-start.8 = (bf16[2,2,2,144,384]{4,3,0,1,2:T(8,128)(2,1)}, bf16[2,2,2,144,384]{4,3,0,1,2:T(8,128)(2,1)}, u32[]{:S(2)}, u32[]{:S(2)}) collective-permute-start(bf16[2,2,2,144,384]{4,3,0,1,2:T(8,128)(2,1)} %copy_bitcast_fusion), channel_id=1, source_target_pairs={{0,1},{1,0},{2,3},{3,2},{4,5},{5,4},{6,7},{7,6},{8,9},{9,8},{10,11... | collective-permute-start | bytes 2654216 | tf_op jit(solution)/shard_map/ppermute | solution.py:1162
  403.6 35.3 %collective-permute-start.9 = (bf16[2,2,320,384]{3,2,1,0:T(8,128)(2,1)S(1)}, bf16[2,2,320,384]{3,2,1,0:T(8,128)(2,1)}, u32[]{:S(2)}, u32[]{:S(2)}) collective-permute-start(bf16[2,2,320,384]{3,2,1,0:T(8,128)(2,1)S(1)} %dynamic-slice_bitcast_fusion), channel_id=1, source_target_pairs={{0,4},{2,6},{4,0},{6,2},{8,12},{10,14},{12,8},{14,10},{16,20},{18,... | collective-permute-start | bytes 2949128 | tf_op jit(solution)/shard_map/ppermute | solution.py:1162
  422.6 16.3 %copy-start.1 = (bf16[8,320,384]{2,1,0:T(8,128)(2,1)S(1)}, bf16[8,320,384]{2,1,0:T(8,128)(2,1)}, u32[]{:S(2)}) copy-start(bf16[8,320,384]{2,1,0:T(8,128)(2,1)} %add_convert_fusion) | copy-start | bytes 5898244
  425.3 15.1 %copy-start.3 = (bf16[2,2,2,144,384]{4,3,0,1,2:T(8,128)(2,1)}, bf16[2,2,2,144,384]{4,3,0,1,2:T(8,128)(2,1)S(1)}, u32[]{:S(2)}) copy-start(bf16[2,2,2,144,384]{4,3,0,1,2:T(8,128)(2,1)S(1)} %fusion.1) | copy-start | bytes 2654212
  441.3 27.8 %collective-permute-start.10 = (bf16[2,2,144,384]{3,2,0,1:T(8,128)(2,1)}, bf16[2,2,144,384]{3,2,0,1:T(8,128)(2,1)S(1)}, u32[]{:S(2)}, u32[]{:S(2)}) collective-permute-start(bf16[2,2,144,384]{3,2,0,1:T(8,128)(2,1)} %dynamic-slice_bitcast_fusion.1), channel_id=1, source_target_pairs={{0,4},{2,6},{4,0},{6,2},{8,12},{10,14},{12,8},{14,10},{16,20},{18,... | collective-permute-start | bytes 1327112 | tf_op jit(solution)/shard_map/ppermute | solution.py:1162
  444.0 22.2 %copy-start.24 = (f32[32,128]{1,0:T(8,128)S(1)}, f32[32,128]{1,0:T(8,128)}, u32[]{:S(2)}) copy-start(f32[32,128]{1,0:T(8,128)} %get-tuple-element.298) | copy-start | bytes 49156
  444.0 22.2 %copy-start.26 = (bf16[128,16]{0,1:T(8,128)(2,1)S(1)}, bf16[128,16]{0,1:T(8,128)(2,1)}, u32[]{:S(2)}) copy-start(bf16[128,16]{0,1:T(8,128)(2,1)} %param.32) | copy-start | bytes 12292
  444.0 22.2 %copy-start.31 = (f32[128]{0:T(128)S(1)}, f32[128]{0:T(128)}, u32[]{:S(2)}) copy-start(f32[128]{0:T(128)} %param.31) | copy-start | bytes 1540
  444.1 24.0 %collective-permute-start.11 = (bf16[2,2,128,384]{3,2,0,1:T(8,128)(2,1)S(1)}, bf16[2,2,128,384]{3,2,0,1:T(8,128)(2,1)}, u32[]{:S(2)}, u32[]{:S(2)}) collective-permute-start(bf16[2,2,128,384]{3,2,0,1:T(8,128)(2,1)S(1)} %bitcast.147), channel_id=1, source_target_pairs={{0,1},{1,0},{2,3},{3,2},{4,5},{5,4},{6,7},{7,6},{8,9},{9,8},{10,11... | collective-permute-start | bytes 1179656 | tf_op jit(solution)/shard_map/ppermute | solution.py:1162
  444.1 22.9 %collective-permute-start.12 = (bf16[2,2,64,384]{3,2,1,0:T(8,128)(2,1)S(1)}, bf16[2,2,64,384]{3,2,1,0:T(8,128)(2,1)}, u32[]{:S(2)}, u32[]{:S(2)}) collective-permute-start(bf16[2,2,64,384]{3,2,1,0:T(8,128)(2,1)S(1)} %slice.138), channel_id=1, source_target_pairs={{0,8},{2,10},{4,12},{6,14},{8,0},{10,2},{12,4},{14,6},{16,24},{18,... | collective-permute-start | bytes 589832 | tf_op jit(solution)/shard_map/ppermute | solution.py:1162
  465.3 3.8 copy-start.4
  471.1 14.0 %collective-permute-start.13 = (bf16[2,272,384]{2,1,0:T(8,128)(2,1)S(1)}, bf16[2,272,384]{2,1,0:T(8,128)(2,1)S(1)}, u32[]{:S(2)}, u32[]{:S(2)}) collective-permute-start(bf16[2,272,384]{2,1,0:T(8,128)(2,1)S(1)} %dynamic-slice_bitcast_fusion.2), channel_id=1, source_target_pairs={{0,8},{2,10},{4,12},{6,14},{8,0},{10,2},{12,4},{14,6},{16,24},{18,... | collective-permute-start | bytes 1253384 | tf_op jit(solution)/shard_map/ppermute | solution.py:1162
  472.6 11.1 %collective-permute-start.14 = (bf16[2,2,64,384]{3,2,1,0:T(8,128)(2,1)S(1)}, bf16[2,2,64,384]{3,2,1,0:T(8,128)(2,1)S(1)}, u32[]{:S(2)}, u32[]{:S(2)}) collective-permute-start(bf16[2,2,64,384]{3,2,1,0:T(8,128)(2,1)S(1)} %add_convert_fusion.4), channel_id=1, source_target_pairs={{0,16},{2,18},{4,20},{6,22},{8,24},{10,26},{12,28},{14,30},{16,0},... | collective-permute-start | bytes 589832 | tf_op jit(solution)/shard_map/ppermute | solution.py:1162
  474.5 1.3 collective-permute-start.15
  475.8 3.9 collective-permute-start.16
  483.8 13.9 %copy-start.18 = (bf16[256,768]{1,0:T(8,128)(2,1)S(1)}, bf16[256,768]{1,0:T(8,128)(2,1)}, u32[]{:S(2)}) copy-start(bf16[256,768]{1,0:T(8,128)(2,1)} %get-tuple-element.189) | copy-start | bytes 1179652
  483.8 13.9 %copy-start.19 = (bf16[256,768]{1,0:T(8,128)(2,1)S(1)}, bf16[256,768]{1,0:T(8,128)(2,1)}, u32[]{:S(2)}) copy-start(bf16[256,768]{1,0:T(8,128)(2,1)} %get-tuple-element.206) | copy-start | bytes 1179652
  485.2 6.1 %collective-permute-start.18 = (bf16[2,2,64,384]{3,2,1,0:T(8,128)(2,1)S(1)}, bf16[2,2,64,384]{3,2,1,0:T(8,128)(2,1)S(1)}, u32[]{:S(2)}, u32[]{:S(2)}) collective-permute-start(bf16[2,2,64,384]{3,2,1,0:T(8,128)(2,1)S(1)} %add_convert_fusion.3), channel_id=1, source_target_pairs={{0,4},{2,6},{4,0},{6,2},{8,12},{10,14},{12,8},{14,10},{16,20},{18,... | collective-permute-start | bytes 589832 | tf_op jit(solution)/shard_map/ppermute | solution.py:1162
  486.8 4.5 collective-permute-start.19
  487.3 10.2 %collective-permute-start.17 = (bf16[272,384]{1,0:T(8,128)(2,1)S(1)}, bf16[272,384]{1,0:T(8,128)(2,1)S(1)}, u32[]{:S(2)}, u32[]{:S(2)}) collective-permute-start(bf16[272,384]{1,0:T(8,128)(2,1)S(1)} %dynamic-slice_bitcast_fusion.3), channel_id=1, source_target_pairs={{0,16},{2,18},{4,20},{6,22},{8,24},{10,26},{12,28},{14,30},{16,0},... | collective-permute-start | bytes 626696 | tf_op jit(solution)/shard_map/ppermute | solution.py:1162
  491.3 7.4 %copy-start.9 = (bf16[1,416,384]{2,1,0:T(8,128)(2,1)S(1)}, bf16[1,416,384]{2,1,0:T(8,128)(2,1)}, u32[]{:S(2)}) copy-start(bf16[1,416,384]{2,1,0:T(8,128)(2,1)} %reduce-scatter.2.cloned.1.call-done) | copy-start | bytes 958468
  497.6 3.9 collective-permute-start.21
  500.8 8.6 %collective-permute-start.20 = (bf16[2,2,2,64,384]{4,3,2,1,0:T(8,128)(2,1)S(1)}, bf16[2,2,2,64,384]{4,3,2,1,0:T(8,128)(2,1)S(1)}, u32[]{:S(2)}, u32[]{:S(2)}) collective-permute-start(bf16[2,2,2,64,384]{4,3,2,1,0:T(8,128)(2,1)S(1)} %pad_maximum_fusion.3), channel_id=1, source_target_pairs={{0,2},{2,0},{4,6},{6,4},{8,10},{10,8},{12,14},{14,12},{16,18},{18,... | collective-permute-start | bytes 1179656 | tf_op jit(solution)/shard_map/ppermute | solution.py:1162
  501.5 4.8 collective-permute-start.22
  (5 other events, 6.7 us)
Sparse Core Ops, SparseCore 0:
  281.8 189.0 reduce-scatter.1
